TPU v7x, 32 devices: a whole 2x2x4 slice. The times are simulated.
32 devices in a mesh: ky: 8 (over y, x, core), kx: 4 (over z).
Axes of the slice: x: 2, y: 2, z: 4, core: 2. Of those that a mesh axis runs over, the one named last changes fastest.
Arguments:
- spectrum: bfloat16 [2, 4096, 2048], P(None, 'ky', 'kx'), may hold values from -6 to 6
- pupil_field: bfloat16 [2, 1024, 1024], replicated, may hold values from -3 to 3
- amplitude: bfloat16 [8192, 4096], P('ky', 'kx'), may hold values from 0 to 2
- offsets: int32 [8, 4, 2], P('ky', 'kx'), may hold values from -384 to 3456, as said below
Outputs:
- spectrum_grad: float32 [2, 4096, 2048], P(None, 'ky', 'kx')
- pupil_grad: float32 [2097152], P(('ky', 'kx'))
Inputs may be any that keep to these rules, and one draw needn't show every extreme that they name: offsets[i, j] = (i * 512 - 512/2 + dy, j * 512 - 512/2 + dx) with whole numbers dy, dx from -128 to 128; both ends of this range are taken in every draw.
All inputs are finite; a program needn't handle non-finite values.
Results may differ from a plain program's by a relative error of at most 0.0028.
Values may be sent and summed in bfloat16 or wider, within the bound.
A program may use at most 192 MiB of HBM per device.

v0:
```python
import math

import jax
import jax.numpy as jnp
from jax import lax
from jax.sharding import PartitionSpec as P

AMP_FLOOR = 0.25


def extended_2(array, sides, width):
    for axis, dim in sides:
        devices, length = (lax.axis_size(axis), array.shape[dim])
        up = [(i, (i + 1) % devices) for i in range(devices - 1)]
        down = [(j, i) for i, j in up]
        last = lax.slice_in_dim(array, length - width, length, axis=dim)
        leading = lax.slice_in_dim(array, 0, width, axis=dim)
        before = lax.ppermute(last, axis, up)
        after = lax.ppermute(leading, axis, down)
        array = jnp.concatenate([before, array, after], axis=dim)
    return array


def factors(length):
    base_size = 128
    return (length // base_size, base_size)


def phase_table(rows_count, cols_count, modulus, angle_sign):
    left_index = jnp.arange(rows_count, dtype=jnp.int32)[:, None]
    right_index = jnp.arange(cols_count, dtype=jnp.int32)[None, :]
    products = left_index * right_index % modulus
    angles = angle_sign * 2.0 * math.pi / modulus * products.astype(jnp.float32)
    return (jnp.cos(angles), jnp.sin(angles))


def block_table(table_real, table_imag):
    first_row = jnp.stack([table_real, table_imag], axis=1)
    second_row = jnp.stack([-table_imag, table_real], axis=1)
    return jnp.stack([first_row, second_row], axis=0)


def complex_section(stacked, table, left_spec, table_spec, out_spec):
    full_form = "p" + left_spec + ",p" + table_spec[0] + "q" + table_spec[1] + "->q" + out_spec
    return jnp.einsum(full_form, stacked, table, precision=lax.Precision.HIGHEST)


def twist(stacked, table_real, table_imag):
    real_part = stacked[0] * table_real - stacked[1] * table_imag
    imag_part = stacked[0] * table_imag + stacked[1] * table_real
    return jnp.stack([real_part, imag_part])


def transform(stacked, angle_sign, along_rows, scrambled_out):
    length = stacked.shape[1]
    size_a, size_b = factors(length)
    short_table = block_table(*phase_table(size_a, size_a, size_a, angle_sign))
    long_table = block_table(*phase_table(size_b, size_b, size_b, angle_sign))
    twist_real, twist_imag = phase_table(size_a, size_b, length, angle_sign)
    if along_rows:
        split_shape = (2, size_a, size_b, length)
        twist_real = twist_real[:, :, None]
        twist_imag = twist_imag[:, :, None]
        if scrambled_out:
            first_forms = ("abw", "ac", "cbw")
            second_forms = ("cbw", "bd", "cdw")
        else:
            first_forms = ("abw", "bd", "adw")
            second_forms = ("adw", "ac", "cdw")
    else:
        split_shape = (2, length, size_a, size_b)
        if scrambled_out:
            first_forms = ("wab", "ac", "wcb")
            second_forms = ("wcb", "bd", "wcd")
        else:
            first_forms = ("wab", "bd", "wad")
            second_forms = ("wad", "ac", "wcd")
    if scrambled_out:
        first_table, second_table = (short_table, long_table)
    else:
        first_table, second_table = (long_table, short_table)
    parts = stacked.reshape(split_shape)
    parts = complex_section(parts, first_table, first_forms[0], first_forms[1], first_forms[2])
    parts = twist(parts, twist_real, twist_imag)
    parts = complex_section(parts, second_table, second_forms[0], second_forms[1], second_forms[2])
    return parts.reshape(2, length, length)


def fold_rims(extended, axis, tile_side, rim_width):
    middle = lax.slice_in_dim(extended, 2 * rim_width, 2 * rim_width + tile_side, axis=axis).astype(
        jnp.float32
    )
    left_rim = lax.slice_in_dim(extended, 0, rim_width, axis=axis).astype(jnp.float32)
    right_rim = lax.slice_in_dim(
        extended, 3 * rim_width + tile_side, 4 * rim_width + tile_side, axis=axis
    ).astype(jnp.float32)
    left_pads = [(0, 0)] * extended.ndim
    right_pads = [(0, 0)] * extended.ndim
    left_pads[axis] = (0, tile_side - rim_width)
    right_pads[axis] = (tile_side - rim_width, 0)
    return middle + jnp.pad(left_rim, left_pads) + jnp.pad(right_rim, right_pads)


def body(spectrum, pupil_field, amplitude, offsets):
    tile_side = spectrum.shape[1]
    rim_width = 3 * tile_side // 4
    win_side = 2 * tile_side
    region = extended_2(spectrum, (("ky", 1), ("kx", 2)), rim_width)
    led_row = lax.axis_index("ky")
    led_col = lax.axis_index("kx")
    row_start = offsets[0, 0, 0] - (led_row * tile_side - rim_width)
    col_start = offsets[0, 0, 1] - (led_col * tile_side - rim_width)
    zero_index = jnp.zeros((), jnp.int32)
    window = lax.dynamic_slice(
        region, (zero_index, row_start, col_start), (2, win_side, win_side)
    ).astype(jnp.float32)
    pupil_real = pupil_field[0].astype(jnp.float32)
    pupil_imag = pupil_field[1].astype(jnp.float32)
    field = jnp.stack(
        [
            pupil_real * window[0] - pupil_imag * window[1],
            pupil_real * window[1] + pupil_imag * window[0],
        ]
    )
    scale = 1.0 / win_side
    image = transform(field, 1.0, False, True)
    image = transform(image, 1.0, True, True) * scale
    size_a, size_b = factors(win_side)
    measured = (
        amplitude.reshape(size_b, size_a, size_b, size_a)
        .transpose(1, 0, 3, 2)
        .reshape(win_side, win_side)
        .astype(jnp.float32)
    )
    magnitude = jnp.sqrt(image[0] * image[0] + image[1] * image[1])
    ratio = measured / jnp.maximum(magnitude, AMP_FLOOR)
    resid = image - ratio[None] * image
    spec = transform(resid, -1.0, False, False)
    spec = transform(spec, -1.0, True, False) * scale
    grad_real = (pupil_real * spec[0] + pupil_imag * spec[1]).astype(jnp.bfloat16)
    grad_imag = (pupil_real * spec[1] - pupil_imag * spec[0]).astype(jnp.bfloat16)
    term_real = window[0] * spec[0] + window[1] * spec[1]
    term_imag = window[0] * spec[1] - window[1] * spec[0]
    led_count = lax.axis_size("ky") * lax.axis_size("kx")
    pupil_terms = jnp.stack([term_real, term_imag]).reshape(-1) / led_count
    pupil_grad = lax.psum_scatter(pupil_terms, ("ky", "kx"), scatter_dimension=0, tiled=True)
    frame_side = tile_side + 2 * rim_width
    frame = jnp.zeros((2, frame_side, frame_side), jnp.bfloat16)
    frame = lax.dynamic_update_slice(
        frame, jnp.stack([grad_real, grad_imag]), (zero_index, row_start, col_start)
    )
    extended = extended_2(frame, (("ky", 1), ("kx", 2)), rim_width)
    spectrum_grad = fold_rims(fold_rims(extended, 1, tile_side, rim_width), 2, tile_side, rim_width)
    return (spectrum_grad, pupil_grad)


def solution(mesh):
    return jax.shard_map(
        body,
        mesh=mesh,
        in_specs=(P(None, "ky", "kx"), P(), P("ky", "kx"), P("ky", "kx", None)),
        out_specs=(P(None, "ky", "kx"), P(("ky", "kx"))),
        check_vma=False,
    )
```

profile of v0, /device:TPU:0, one launch (start us, length us, event | category | flops | bytes accessed | tf_op | source)
XLA Modules:
  0.0 612.7 jit_solution(7379108351449086506)
XLA Ops:
  28.4 42.2 %reshape.376 = f32[128,8,128,8]{3,2,1,0:T(8,128)} reshape(bf16[1024,1024]{1,0:T(8,128)(2,1)} %param.6) | data formatting | bytes 6291456 | tf_op jit(solution)/shard_map/convert_element_type | solution.py:133
  70.6 35.0 %copy.76 = f32[8,128,8,128]{3,2,1,0:T(8,128)} copy(f32[8,128,8,128]{2,3,0,1:T(8,128)} %bitcast.38) | data formatting | bytes 8388608 | tf_op jit(solution)/shard_map/convert_element_type | solution.py:133
  112.0 6.3 %fusion.32 = f32[2,1024,1024]{2,1,0:T(8,128)S(1)} fusion(s32[]{:T(128)S(6)} %select_n.185, s32[]{:T(128)S(6)} %select_n.186, bf16[2,1280,384]{2,1,0:T(8,128)(2,1)} %collective-permute-done.2, bf16[2,1280,512]{2,1,0:T(8,128)(2,1)S(1)} %constant_dynamic-update-slice_fusion, bf16[2,1280,384]{2,1,0:T(8,128)(2,1)} %collective-permute-done.3), kind=kLoop, calls=%fused_computation.53 | loop fusion | flops 12582912 | bytes 14942216 | tf_op jit(solution)/shard_map/convert_element_type | solution.py:116
  124.6 8.1 %fusion.68 = f32[2,1024,8,128]{3,2,1,0:T(8,128)S(1)} fusion(f32[1,1024,8,128]{3,2,0,1:T(8,128)S(1)} %bitcast.185, f32[1,1024,8,128]{3,2,0,1:T(8,128)S(1)} %bitcast.184, f32[1,8,2,8]{1,3,0,2:T(8,128)S(1)} %copy.69, f32[1,8,2,8]{1,3,0,2:T(8,128)S(1)} %copy.68), kind=kOutput, calls=%fused_computation.96 | convolution fusion | flops 404750592 | bytes 16778240 | tf_op jit(solution)/shard_map/pwab,paqc->qwcb/dot_general | solution.py:45
  134.1 9.7 %fusion.20 = f32[2,128,1024,8,1]{2,1,4,3,0:T(8,128)S(1)} fusion(f32[2,1024,8,128]{3,2,1,0:T(8,128)S(1)} %pad_maximum_fusion, f32[1,128,2,128]{1,3,0,2:T(8,128)S(1)} %get-tuple-element.31, f32[1,128,2,128]{1,3,0,2:T(8,128)S(1)} %get-tuple-element.30), kind=kOutput, calls=%fused_computation.28 | convolution fusion | flops 6442516480 | bytes 17039360 | tf_op jit(solution)/shard_map/pwcb,pbqd->qwcd/dot_general | solution.py:45
  143.9 5.3 copy.104
  149.2 8.8 %copy.71 = f32[2,8,128,1024]{3,1,0,2:T(8,128)} copy(f32[2,8,128,1024]{2,1,3,0:T(8,128)} %bitcast.182) | data formatting | bytes 16777216 | tf_op jit(solution)/shard_map/reshape;reshape | solution.py:82
  158.0 11.7 %fusion.56 = f32[2,8,128,1024]{3,1,2,0:T(8,128)S(1)} fusion(f32[2,8,128,1024]{3,1,0,2:T(8,128)} %copy.71, f32[1,8,2,8]{1,3,0,2:T(8,128)S(1)} %copy.69, f32[1,8,2,8]{1,3,0,2:T(8,128)S(1)} %copy.68), kind=kOutput, calls=%fused_computation.92 | convolution fusion | flops 402653440 | bytes 16778240 | tf_op jit(solution)/shard_map/pabw,paqc->qcbw/dot_general | solution.py:45
  172.5 13.1 %bitcast_multiply_fusion = (f32[2,8,128,1024]{3,2,1,0:T(8,128)}, f32[2,128,8,1024,1]{3,1,4,2,0:T(8,128)S(1)}) fusion(f32[2,8,128,1024]{3,1,2,0:T(8,128)S(1)} %pad_maximum_fusion.1, f32[1,128,2,128]{1,3,0,2:T(8,128)S(1)} %get-tuple-element.31, f32[1,128,2,128]{1,3,0,2:T(8,128)S(1)} %get-tuple-element.30), kind=kOutput, calls=%fused_computation.23 | convolution fusion | flops 6444613632 | bytes 25427968 | tf_op jit(solution)/shard_map/pcbw,pbqd->qcdw/dot_general | solution.py:45
  185.6 5.1 fusion.47
  195.6 10.0 %fusion.65 = f32[2,1024,8,128]{1,3,2,0:T(8,128)S(1)} fusion(f32[2,1024,8,128]{3,2,1,0:T(8,128)S(1)} %bitcast.183, f32[1024,8,128]{2,0,1:T(8,128)S(1)} %copy.77, f32[1,128,2,128]{1,3,2,0:T(8,128)S(1)} %get-tuple-element.29, f32[1,128,2,128]{1,3,2,0:T(8,128)S(1)} %get-tuple-element.28), kind=kOutput, calls=%fused_computation.95 | convolution fusion | flops 6448807936 | bytes 21233664 | tf_op jit(solution)/shard_map/pwab,pbqd->qwad/dot_general | solution.py:45
  210.9 9.2 %copy.80 = f32[2,1024,8,128]{3,2,0,1:T(8,128)} copy(f32[2,1024,8,128]{1,3,2,0:T(8,128)} %pad_maximum_fusion.2) | data formatting | bytes 16777216 | tf_op jit(solution)/shard_map/stack | solution.py:51
  220.0 12.1 %fusion.59 = f32[2,1024,8,128]{3,2,1,0:T(8,128)} fusion(f32[2,1024,8,128]{3,2,0,1:T(8,128)} %copy.80, f32[1,8,2,8]{1,3,0,2:T(8,128)S(1)} %copy.66, f32[1,8,2,8]{1,3,0,2:T(8,128)S(1)} %copy.65), kind=kOutput, calls=%fused_computation.93 | convolution fusion | flops 402653440 | bytes 16778240 | tf_op jit(solution)/shard_map/pwad,paqc->qwcd/dot_general | solution.py:45
  232.2 9.2 %reshape_reshape.7 = f32[2,8,128,1024]{3,2,1,0:T(8,128)} reshape(f32[2,1024,8,128]{3,2,1,0:T(8,128)} %fusion.59) | data formatting | bytes 16777216 | tf_op jit(solution)/shard_map/reshape;reshape | solution.py:82
  241.4 9.7 %fusion.53 = f32[2,8,128,1024]{3,2,1,0:T(8,128)S(1)} fusion(f32[2,8,128,1024]{3,2,1,0:T(8,128)} %reshape_reshape.7, f32[1,128,2,128]{1,3,2,0:T(8,128)S(1)} %get-tuple-element.29, f32[1,128,2,128]{1,3,2,0:T(8,128)S(1)} %get-tuple-element.28), kind=kOutput, calls=%fused_computation.91 | convolution fusion | flops 6442516480 | bytes 17039360 | tf_op jit(solution)/shard_map/pabw,pbqd->qadw/dot_general | solution.py:45
  254.1 12.0 %fusion.62 = f32[2,8,128,1024]{3,1,2,0:T(8,128)S(1)} fusion(f32[2,8,128,1024]{3,2,1,0:T(8,128)S(1)} %pad_maximum_fusion.3, f32[1,8,2,8]{1,3,0,2:T(8,128)S(1)} %copy.66, f32[1,8,2,8]{1,3,0,2:T(8,128)S(1)} %copy.65), kind=kOutput, calls=%fused_computation.94 | convolution fusion | flops 402653440 | bytes 16778240 | tf_op jit(solution)/shard_map/padw,paqc->qcdw/dot_general | solution.py:45
  266.1 8.5 %copy_multiply_fusion = f32[2,8,128,1024]{3,2,1,0:T(8,128)} fusion(f32[2,8,128,1024]{3,1,2,0:T(8,128)S(1)} %fusion.62), kind=kLoop, calls=%fused_computation.30 | loop fusion | flops 2097152 | bytes 16777216 | tf_op jit(solution)/shard_map/mul | solution.py:139
  280.6 7.2 %fusion.48 = (f32[1,1024,1024]{2,1,0:T(8,128)}, f32[1,1024,1024]{2,1,0:T(8,128)}, bf16[1,1024,1024]{2,1,0:T(8,128)(2,1)}, bf16[1,1024,1024]{2,1,0:T(8,128)(2,1)}) fusion(f32[1,8,128,1024]{3,2,1,0:T(8,128)S(1)} %get-tuple-element.21, f32[1,8,128,1024]{3,2,1,0:T(8,128)S(1)} %get-tuple-element.20, f32[2,1024,1024]{2,1,0:T(8,128)S(1)} %bitcast.177, ...), kind=kLoop, calls=%fused_computation.75 | loop fusion | flops 16777216 | bytes 33554432 | tf_op jit(solution)/shard_map/add | solution.py:142
  295.6 45.7 %dynamic_update_slice.3 = bf16[2,1280,1280]{2,1,0:T(8,128)(2,1)} dynamic-update-slice(bf16[2,1280,1280]{2,1,0:T(8,128)(2,1)} %broadcast_in_dim.2, bf16[2,1024,1024]{2,1,0:T(8,128)(2,1)} %pad_maximum_fusion.4, s32[]{:T(128)} %constant.93.clone.1, s32[]{:T(128)S(6)} %select_n.185, s32[]{:T(128)S(6)} %select_n.186) | dynamic-update-slice | bytes 8388612 | tf_op jit(solution)/shard_map/dynamic_update_slice | solution.py:149
  345.8 17.4 %collective-permute-start.4 = (bf16[2,384,1280]{2,1,0:T(8,128)(2,1)}, bf16[2,384,1280]{2,1,0:T(8,128)(2,1)S(1)}, u32[]{:S(2)}, u32[]{:S(2)}) collective-permute-start(bf16[2,384,1280]{2,1,0:T(8,128)(2,1)} %get-tuple-element.22), channel_id=1, source_target_pairs={{0,4},{4,8},{8,12},{12,16},{16,20},{20,24},{24,28},{1,5},{5,9},{9,... | collective-permute-start | bytes 5898248 | tf_op jit(solution)/shard_map/ppermute | solution.py:18
  368.4 5.3 copy.107
  378.5 6.0 collective-permute-start.6
  385.8 199.3 %all-reduce.5.cloned.1.call-done = f32[2097152]{0:T(1024)} async-done(((f32[2097152]{0:T(1024)}), f32[2097152]{0:T(1024)}) %all-reduce.5.cloned.1.call-update) | async-done | bytes 8388624
  586.7 16.7 %convert_add_fusion = f32[2,512,2048]{2,1,0:T(8,128)S(1)} fusion(bf16[2,2048,384]{2,1,0:T(8,128)(2,1)} %collective-permute-done.7, bf16[2,2048,384]{2,1,0:T(8,128)(2,1)} %collective-permute-done.6, bf16[2,384,1280]{2,1,0:T(8,128)(2,1)} %collective-permute-done.5, bf16[2,1280,1280]{2,1,0:T(8,128)(2,1)} %dynamic_update_slice.3, ...), kind=kLoop, calls=%fused_computation.35 | loop fusion | flops 83886080 | bytes 25166336 | tf_op jit(solution)/shard_map/add | solution.py:101
  (88 shorter events, 82.7 us)
Async XLA Ops:
  7.2 577.9 %all-reduce.5.cloned.1.call-start = ((), (), s32[]{:S(2)}) async-start(), calls=%async_computation | async-start | bytes 16777216
  7.2 5.9 copy-start.5
  8.8 4.3 collective-permute-start
  11.2 6.2 %collective-permute-start.1 = (bf16[2,384,512]{2,1,0:T(8,128)(2,1)S(1)}, bf16[2,384,512]{2,1,0:T(8,128)(2,1)S(1)}, u32[]{:S(2)}, u32[]{:S(2)}) collective-permute-start(bf16[2,384,512]{2,1,0:T(8,128)(2,1)S(1)} %get-tuple-element.26), channel_id=1, source_target_pairs={{4,0},{8,4},{12,8},{16,12},{20,16},{24,20},{28,24},{5,1},{9,5},{13... | collective-permute-start | bytes 2359304 | tf_op jit(solution)/shard_map/ppermute | solution.py:19
  17.5 8.5 %copy-start.7 = (s32[1,1,2]{2,1,0:T(1,128)S(1)}, s32[1,1,2]{2,1,0:T(1,128)}, u32[]{:S(2)}) copy-start(s32[1,1,2]{2,1,0:T(1,128)} %param.7) | copy-start | bytes 28
  19.9 92.1 %collective-permute-start.2 = (bf16[2,1280,384]{2,1,0:T(8,128)(2,1)}, bf16[2,1280,384]{2,1,0:T(8,128)(2,1)}, u32[]{:S(2)}, u32[]{:S(2)}) collective-permute-start(bf16[2,1280,384]{2,1,0:T(8,128)(2,1)} %get-tuple-element.25), channel_id=1, source_target_pairs={{0,1},{1,2},{2,3},{4,5},{5,6},{6,7},{8,9},{9,10},{10,11},{12,13},{... | collective-permute-start | bytes 5898248 | tf_op jit(solution)/shard_map/ppermute | solution.py:18
  24.7 87.4 %collective-permute-start.3 = (bf16[2,1280,384]{2,1,0:T(8,128)(2,1)}, bf16[2,1280,384]{2,1,0:T(8,128)(2,1)}, u32[]{:S(2)}, u32[]{:S(2)}) collective-permute-start(bf16[2,1280,384]{2,1,0:T(8,128)(2,1)} %get-tuple-element.24), channel_id=1, source_target_pairs={{1,0},{2,1},{3,2},{5,4},{6,5},{7,6},{9,8},{10,9},{11,10},{13,12},{... | collective-permute-start | bytes 5898248 | tf_op jit(solution)/shard_map/ppermute | solution.py:19
  112.0 6.3 %copy-start.2 = (bf16[2,1024,1024]{2,1,0:T(8,128)(2,1)S(1)}, bf16[2,1024,1024]{2,1,0:T(8,128)(2,1)}, u32[]{:S(2)}) copy-start(bf16[2,1024,1024]{2,1,0:T(8,128)(2,1)} %param.5) | copy-start | bytes 12582916
  118.3 4.3 copy-start
  185.6 5.1 copy-start.1
  266.1 13.0 %slice-start = ((s8[8388608]{0:T(1024)(128)(4,1)}), s8[4194304]{0:T(1024)(128)(4,1)S(1)}, s32[]{:S(2)}) async-start(s8[8388608]{0:T(1024)(128)(4,1)} %bitcast.176), calls=%async_computation.1 | async-start | bytes 8388608
  274.6 4.6 slice-start.1
  274.7 5.9 copy-start.3
  341.3 23.5 %copy-start.4 = (f32[1,1024,1024]{2,1,0:T(8,128)S(1)}, f32[1,1024,1024]{2,1,0:T(8,128)}, u32[]{:S(2)}) copy-start(f32[1,1024,1024]{2,1,0:T(8,128)} %get-tuple-element.2) | copy-start | bytes 12582916
  345.8 28.0 %collective-permute-start.4 = (bf16[2,384,1280]{2,1,0:T(8,128)(2,1)}, bf16[2,384,1280]{2,1,0:T(8,128)(2,1)S(1)}, u32[]{:S(2)}, u32[]{:S(2)}) collective-permute-start(bf16[2,384,1280]{2,1,0:T(8,128)(2,1)} %get-tuple-element.22), channel_id=1, source_target_pairs={{0,4},{4,8},{8,12},{12,16},{16,20},{20,24},{24,28},{1,5},{5,9},{9,... | collective-permute-start | bytes 5898248 | tf_op jit(solution)/shard_map/ppermute | solution.py:18
  363.3 10.6 %collective-permute-start.5 = (bf16[2,384,1280]{2,1,0:T(8,128)(2,1)}, bf16[2,384,1280]{2,1,0:T(8,128)(2,1)}, u32[]{:S(2)}, u32[]{:S(2)}) collective-permute-start(bf16[2,384,1280]{2,1,0:T(8,128)(2,1)} %get-tuple-element.23), channel_id=1, source_target_pairs={{4,0},{8,4},{12,8},{16,12},{20,16},{24,20},{28,24},{5,1},{9,5},{13... | collective-permute-start | bytes 5898248 | tf_op jit(solution)/shard_map/ppermute | solution.py:19
  373.8 212.9 %copy-start.6 = (pred[512]{0:T(512)(128)(4,1)S(1)}, pred[512]{0:T(512)(128)(4,1)}, u32[]{:S(2)}) copy-start(pred[512]{0:T(512)(128)(4,1)} %constant.114.clone.1) | copy-start | bytes 1540
  378.5 208.2 %collective-permute-start.6 = (bf16[2,2048,384]{2,1,0:T(8,128)(2,1)}, bf16[2,2048,384]{2,1,0:T(8,128)(2,1)}, u32[]{:S(2)}, u32[]{:S(2)}) collective-permute-start(bf16[2,2048,384]{2,1,0:T(8,128)(2,1)} %get-tuple-element.8), channel_id=1, source_target_pairs={{0,1},{1,2},{2,3},{4,5},{5,6},{6,7},{8,9},{9,10},{10,11},{12,13},{... | collective-permute-start | bytes 9437192 | tf_op jit(solution)/shard_map/ppermute | solution.py:18
  384.5 202.3 %collective-permute-start.7 = (bf16[2,2048,384]{2,1,0:T(8,128)(2,1)}, bf16[2,2048,384]{2,1,0:T(8,128)(2,1)}, u32[]{:S(2)}, u32[]{:S(2)}) collective-permute-start(bf16[2,2048,384]{2,1,0:T(8,128)(2,1)} %get-tuple-element.9), channel_id=1, source_target_pairs={{1,0},{2,1},{3,2},{5,4},{6,5},{7,6},{9,8},{10,9},{11,10},{13,12},{... | collective-permute-start | bytes 9437192 | tf_op jit(solution)/shard_map/ppermute | solution.py:19
Sparse Core Ops, SparseCore 0:
  373.9 211.1 all-reduce.4
where the time goes:
time: 622 us; the launch traced here: 613 us
  waiting for transfers between devices  204 us (33%)
  local copies, waits for them, and re-layouts  194 us (31%)
  matrix products  86.5 us (14%)
  other arithmetic  75.7 us (12%)
  starting transfers between devices  36 us (6%)
  between operations  16.3 us (3%)
    unnamed x2, waiting for transfers between devices  199 us
    dot_general x8, matrix products, complex_section(): jnp.einsum(full_form, stacked, table, precision=lax.Precision.HIGHEST)  86.5 us
    convert_element_type x3, local copies, waits for them, and re-layouts, body(): measured = amplitude.reshape(size_b, size_a, size_b, size_a).transpose(1,...  82.2 us
    dynamic_update_slice x1, local copies, waits for them, and re-layouts, body(): lax.dynamic_update_slice(frame, jnp.stack([grad_real, grad_imag]), (zero_...  45.7 us
    ppermute x4, starting transfers between devices, extended_2(): before = lax.ppermute(last, axis, up)  30.6 us
    unnamed x29, local copies, waits for them, and re-layouts  20.8 us
    add x2, other arithmetic, fold_rims(): middle + jnp.pad(left_rim, left_pads) + jnp.pad(right_rim, right_pads)  18.5 us
    another operation x2, local copies, waits for them, and re-layouts, transform(): parts = stacked.reshape(split_shape)  18 us
  transfers between devices with their start and end apart: 9, of which 3 were waited for; matrix products, arithmetic and copies ran while one was open for 16% of the time, Pallas kernels for 0%

commit v1 on v0

v1 whole, which is shorter than its diff:
```python
import functools
import math

import jax
import jax.numpy as jnp
import ml_dtypes
import numpy as np
from jax import lax
from jax.experimental import pallas as pl
from jax.experimental.pallas import tpu as pltpu
from jax.sharding import PartitionSpec as P

WIN = 1024
A, B = 8, 128
RB = 64
SUB = 16
HALF_ROOT = math.sqrt(0.5)
BF = jnp.bfloat16
F32 = jnp.float32


def make_tables():
    k = np.arange(B)
    ang = 2.0 * np.pi * (np.outer(k, k) % B) / B
    c, s = np.cos(ang) / 32.0, np.sin(ang) / 32.0
    out = []
    for sign in (1.0, -1.0):
        m = np.block([[c, sign * s], [-sign * s, c]])
        hi = m.astype(np.float32).astype(ml_dtypes.bfloat16)
        lo = (m - hi.astype(np.float64)).astype(np.float32).astype(ml_dtypes.bfloat16)
        out.append(np.concatenate([hi, hi, lo], axis=0))
    lane = np.stack(out)
    rows = np.ascontiguousarray(lane.transpose(0, 2, 1))
    ang = 2.0 * np.pi * np.outer(np.arange(A), k) / WIN
    tw = np.stack([np.cos(ang), np.sin(ang)]).astype(np.float32)
    tw_rows = np.ascontiguousarray(np.broadcast_to(tw[:, :, :, None], (2, A, B, 128)))
    return lane, rows, tw, tw_rows


def cadd(x, y):
    return (x[0] + y[0], x[1] + y[1])


def csub(x, y):
    return (x[0] - y[0], x[1] - y[1])


def turn(x, sign):
    return (-x[1], x[0]) if sign > 0 else (x[1], -x[0])


def dft4(x0, x1, x2, x3, sign):
    s, d = cadd(x0, x2), csub(x0, x2)
    t, u = cadd(x1, x3), turn(csub(x1, x3), sign)
    return [cadd(s, t), cadd(d, u), csub(s, t), csub(d, u)]


def dft8(x, sign):
    e = dft4(x[0], x[2], x[4], x[6], sign)
    o = dft4(x[1], x[3], x[5], x[7], sign)
    o1 = cadd(o[1], turn(o[1], sign))
    o1 = (o1[0] * HALF_ROOT, o1[1] * HALF_ROOT)
    o2 = turn(o[2], sign)
    o3 = csub(turn(o[3], sign), o[3])
    o3 = (o3[0] * HALF_ROOT, o3[1] * HALF_ROOT)
    o = [o[0], o1, o2, o3]
    return [cadd(e[k], o[k]) for k in range(4)] + [csub(e[k], o[k]) for k in range(4)]


def split(x):
    hi = x.astype(BF)
    return hi, (x - hi.astype(F32)).astype(BF)


def mul_tw(x, tr, ti, sign):
    if sign > 0:
        return (x[0] * tr - x[1] * ti, x[0] * ti + x[1] * tr)
    return (x[0] * tr + x[1] * ti, x[1] * tr - x[0] * ti)


def kernel(
    inv_leds, starts, region, pupil, amp, lane_t, row_t, tw, tw_rows,
    frame, term, win, fld, lhs, rhs, out_l, out_r, gs,
):
    side = region.shape[1]
    row0, col0 = starts[0], starts[1]
    n_blocks = WIN // RB
    n_sub = RB // SUB

    def pass1(i, carry):
        r0 = row0 + i * RB
        base = jnp.minimum((r0 // 16) * 16, side - RB - 16)
        rem = r0 - base
        rows = pl.ds(pl.multiple_of(i * RB, RB), RB)
        for q in range(2):
            x = region[q, pl.ds(pl.multiple_of(base, 16), RB + 16), :].astype(F32)
            x = pltpu.roll(x, RB + 16 - rem, 0)[:RB]
            x = pltpu.roll(x, side - col0, 1)[:, :WIN]
            win[q, rows, :] = x.astype(BF)
        for s in range(n_sub):
            r = pl.ds(pl.multiple_of(i * RB + s * SUB, SUB), SUB)
            xs = []
            for a in range(A):
                cols = pl.ds(a * B, B)
                pr, pi = pupil[0, r, cols].astype(F32), pupil[1, r, cols].astype(F32)
                wr, wi = win[0, r, cols].astype(F32), win[1, r, cols].astype(F32)
                xs.append((pr * wr - pi * wi, pr * wi + pi * wr))
            ys = dft8(xs, 1)
            for c in range(A):
                y = ys[c]
                if c > 0:
                    y = mul_tw(y, tw[0, c : c + 1, :], tw[1, c : c + 1, :], 1)
                o = pl.ds(c * RB + s * SUB, SUB)
                for q in range(2):
                    hi, lo = split(y[q])
                    lhs[o, q * B : (q + 1) * B] = hi
                    lhs[o, (2 + q) * B : (3 + q) * B] = lo
        out_l[...] = jnp.dot(lhs[...], lane_t[0, :512, :], preferred_element_type=F32) + jnp.dot(
            lhs[:, :256], lane_t[0, 512:, :], preferred_element_type=F32
        )
        for c in range(A):
            for q in range(2):
                fld[q, rows, c * B : (c + 1) * B] = out_l[c * RB : (c + 1) * RB, q * B : (q + 1) * B]
        return carry

    lax.fori_loop(0, n_blocks, pass1, 0)

    def pass2(j, carry):
        cols = pl.ds(pl.multiple_of(j * B, B), B)
        for s in range(B // SUB):
            xs = [
                tuple(fld[q, a * B + s * SUB : a * B + (s + 1) * SUB, cols] for q in range(2))
                for a in range(A)
            ]
            ys = dft8(xs, 1)
            sl = slice(s * SUB, (s + 1) * SUB)
            for c in range(A):
                y = ys[c]
                if c > 0:
                    y = mul_tw(y, tw_rows[0, c, sl, :], tw_rows[1, c, sl, :], 1)
                for q in range(2):
                    hi, lo = split(y[q])
                    rhs[q * B + s * SUB : q * B + (s + 1) * SUB, c * B : (c + 1) * B] = hi
                    rhs[(2 + q) * B + s * SUB : (2 + q) * B + (s + 1) * SUB, c * B : (c + 1) * B] = lo
        out_r[...] = jnp.dot(row_t[0, :, :512], rhs[...], preferred_element_type=F32) + jnp.dot(
            row_t[0, :, 512:], rhs[:256, :], preferred_element_type=F32
        )
        for c in range(A):
            cc = slice(c * B, (c + 1) * B)
            for s in range(B // SUB):
                sl = slice(s * SUB, (s + 1) * SUB)
                zr = out_r[sl, cc]
                zi = out_r[B + s * SUB : B + (s + 1) * SUB, cc]
                m = amp[c * B + s * SUB : c * B + (s + 1) * SUB, cols].astype(F32)
                g = 1.0 - m * lax.rsqrt(jnp.maximum(zr * zr + zi * zi, 0.0625))
                for q, z in enumerate((zr * g, zi * g)):
                    hi, lo = split(z)
                    rhs[q * B + s * SUB : q * B + (s + 1) * SUB, cc] = hi
                    rhs[(2 + q) * B + s * SUB : (2 + q) * B + (s + 1) * SUB, cc] = lo
        out_r[...] = jnp.dot(row_t[1, :, :512], rhs[...], preferred_element_type=F32) + jnp.dot(
            row_t[1, :, 512:], rhs[:256, :], preferred_element_type=F32
        )
        for s in range(B // SUB):
            sl = slice(s * SUB, (s + 1) * SUB)
            ys = []
            for c in range(A):
                cc = slice(c * B, (c + 1) * B)
                y = (out_r[sl, cc], out_r[B + s * SUB : B + (s + 1) * SUB, cc])
                if c > 0:
                    y = mul_tw(y, tw_rows[0, c, sl, :], tw_rows[1, c, sl, :], -1)
                ys.append(y)
            xs = dft8(ys, -1)
            for a in range(A):
                for q in range(2):
                    fld[q, a * B + s * SUB : a * B + (s + 1) * SUB, cols] = xs[a][q]
        return carry

    lax.fori_loop(0, WIN // B, pass2, 0)

    pad = side - WIN
    gs[:, :pad, :] = jnp.zeros((2, pad, side), BF)
    gs[:, pad + WIN :, :] = jnp.zeros((2, pad, side), BF)
    gs[:, pad : pad + WIN, WIN:] = jnp.zeros((2, WIN, pad), BF)

    def pass3(i, carry):
        rows = pl.ds(pl.multiple_of(i * RB, RB), RB)
        for c in range(A):
            for q in range(2):
                hi, lo = split(fld[q, rows, c * B : (c + 1) * B])
                lhs[c * RB : (c + 1) * RB, q * B : (q + 1) * B] = hi
                lhs[c * RB : (c + 1) * RB, (2 + q) * B : (3 + q) * B] = lo
        out_l[...] = jnp.dot(lhs[...], lane_t[1, :512, :], preferred_element_type=F32) + jnp.dot(
            lhs[:, :256], lane_t[1, 512:, :], preferred_element_type=F32
        )
        for s in range(n_sub):
            r = pl.ds(pl.multiple_of(i * RB + s * SUB, SUB), SUB)
            rg = pl.ds(pl.multiple_of(pad + i * RB + s * SUB, SUB), SUB)
            ys = []
            for c in range(A):
                o = slice(c * RB + s * SUB, c * RB + (s + 1) * SUB)
                y = (out_l[o, :B], out_l[o, B:])
                if c > 0:
                    y = mul_tw(y, tw[0, c : c + 1, :], tw[1, c : c + 1, :], -1)
                ys.append(y)
            xs = dft8(ys, -1)
            for a in range(A):
                cols = pl.ds(a * B, B)
                sr, si = xs[a]
                pr, pi = pupil[0, r, cols].astype(F32), pupil[1, r, cols].astype(F32)
                wr, wi = win[0, r, cols].astype(F32), win[1, r, cols].astype(F32)
                gs[0, rg, cols] = (pr * sr + pi * si).astype(BF)
                gs[1, rg, cols] = (pr * si - pi * sr).astype(BF)
                term[0, r, cols] = (wr * sr + wi * si) * inv_leds
                term[1, r, cols] = (wr * si - wi * sr) * inv_leds
        return carry

    lax.fori_loop(0, n_blocks, pass3, 0)

    def pass4(k, carry):
        r0 = k * RB + pad - row0
        base = jnp.minimum((r0 // 16) * 16, gs.shape[1] - RB - 16)
        rem = r0 - base
        for q in range(2):
            x = gs[q, pl.ds(pl.multiple_of(base, 16), RB + 16), :].astype(F32)
            x = pltpu.roll(x, RB + 16 - rem, 0)[:RB]
            x = pltpu.roll(x, col0, 1)
            frame[q, pl.ds(pl.multiple_of(k * RB, RB), RB), :] = x.astype(BF)
        return carry

    lax.fori_loop(0, side // RB, pass4, 0)


def compute(starts, region, pupil, amp, n_leds):
    side = region.shape[1]
    pad = side - WIN
    lane, rows, tw, tw_rows = make_tables()
    vm = pl.BlockSpec(memory_space=pltpu.VMEM)
    return pl.pallas_call(
        functools.partial(kernel, 1.0 / n_leds),
        out_shape=(
            jax.ShapeDtypeStruct((2, side, side), BF),
            jax.ShapeDtypeStruct((2, WIN, WIN), F32),
        ),
        in_specs=[pl.BlockSpec(memory_space=pltpu.SMEM)] + [vm] * 7,
        out_specs=(vm, vm),
        scratch_shapes=[
            pltpu.VMEM((2, WIN, WIN), BF),
            pltpu.VMEM((2, WIN, WIN), F32),
            pltpu.VMEM((A * RB, 512), BF),
            pltpu.VMEM((512, WIN), BF),
            pltpu.VMEM((A * RB, 256), F32),
            pltpu.VMEM((256, WIN), F32),
            pltpu.VMEM((2, WIN + 2 * pad, side), BF),
        ],
        compiler_params=pltpu.CompilerParams(vmem_limit_bytes=60 * 1024 * 1024),
        cost_estimate=pl.CostEstimate(flops=13_000_000_000, bytes_accessed=30_000_000, transcendentals=1_000_000),
    )(starts, region, pupil, amp, jnp.asarray(lane), jnp.asarray(rows), jnp.asarray(tw), jnp.asarray(tw_rows))


def shift(x, axis, step):
    n = lax.axis_size(axis)
    pairs = [(i, i + step) for i in range(n) if 0 <= i + step < n]
    return lax.ppermute(x, axis, pairs)


def gather_region(tile, rim):
    t = tile.shape[1]
    left = shift(tile[:, :, t - rim :], "kx", 1)
    right = shift(tile[:, :, :rim], "kx", -1)
    up = shift(tile[:, t - rim :, :], "ky", 1)
    down = shift(tile[:, :rim, :], "ky", -1)
    sides = jnp.concatenate([left, right], axis=2)
    up_s = shift(sides[:, t - rim :, :], "ky", 1)
    down_s = shift(sides[:, :rim, :], "ky", -1)
    top = jnp.concatenate([up_s[:, :, :rim], up, up_s[:, :, rim:]], axis=2)
    mid = jnp.concatenate([left, tile, right], axis=2)
    bottom = jnp.concatenate([down_s[:, :, :rim], down, down_s[:, :, rim:]], axis=2)
    return jnp.concatenate([top, mid, bottom], axis=1)


def fold_rows(mid, from_up, from_down, rim):
    t = mid.shape[1]
    gap = t - rim
    x = mid.astype(F32)
    x = x + jnp.pad(from_up.astype(F32), ((0, 0), (0, gap), (0, 0)))
    return x + jnp.pad(from_down.astype(F32), ((0, 0), (gap, 0), (0, 0)))


def scatter_frame(frame, t, rim):
    lo, hi = rim, rim + t
    sides = jnp.concatenate([frame[:, :, :lo], frame[:, :, hi:]], axis=2)
    from_down_s = shift(sides[:, :lo, :], "ky", -1)
    from_up_s = shift(sides[:, hi:, :], "ky", 1)
    from_down = shift(frame[:, :lo, lo:hi], "ky", -1)
    from_up = shift(frame[:, hi:, lo:hi], "ky", 1)
    sides = fold_rows(sides[:, lo:hi, :], from_up_s, from_down_s, rim).astype(BF)
    from_right = shift(sides[:, :, :rim], "kx", -1)
    from_left = shift(sides[:, :, rim:], "kx", 1)
    out = fold_rows(frame[:, lo:hi, lo:hi], from_up, from_down, rim)
    gap = t - rim
    out = out + jnp.pad(from_left.astype(F32), ((0, 0), (0, 0), (0, gap)))
    return out + jnp.pad(from_right.astype(F32), ((0, 0), (0, 0), (gap, 0)))


def halve(x, dim, axis, weight, dtype):
    n = lax.axis_size(axis)
    bit = (lax.axis_index(axis) // weight) % 2
    keep = lax.dynamic_index_in_dim(x, bit, dim, keepdims=False)
    send = lax.dynamic_index_in_dim(x, 1 - bit, dim, keepdims=False).astype(dtype)
    got = lax.ppermute(send, axis, [(i, i ^ weight) for i in range(n)])
    return keep + got.astype(F32)


def reduce_terms(term):
    n_ky, n_kx = lax.axis_size("ky"), lax.axis_size("kx")
    bits_y, bits_x = n_ky.bit_length() - 1, n_kx.bit_length() - 1
    rows = 2 * WIN // (n_ky * n_kx)
    half = rows // 2
    flat = term.reshape([2] * (bits_y + bits_x) + [rows, WIN])

    def chain(x, order):
        left = list(range(bits_y + bits_x))
        for step, b in enumerate(order):
            dim = left.index(b)
            left.remove(b)
            axis, weight = ("ky", 1 << (bits_y - 1 - b)) if b < bits_y else ("kx", 1 << (bits_y + bits_x - 1 - b))
            x = halve(x, dim, axis, weight, BF if 1 <= step <= 4 else F32)
        return x

    core = [bits_y - 1]
    y_bits = list(range(bits_y - 2, -1, -1))
    x_bits = list(range(bits_y + bits_x - 1, bits_y - 1, -1))
    first = chain(flat[..., :half, :], core + y_bits + x_bits)
    second = chain(flat[..., half:, :], core + y_bits[::-1] + x_bits)
    return jnp.concatenate([first, second], axis=0).reshape(-1)


def body(spectrum, pupil_field, amplitude, offsets):
    t = spectrum.shape[1]
    rim = 3 * t // 4
    row_start = offsets[0, 0, 0] - (lax.axis_index("ky") * t - rim)
    col_start = offsets[0, 0, 1] - (lax.axis_index("kx") * t - rim)
    starts = jnp.stack([row_start, col_start]).astype(jnp.int32)
    k = jnp.arange(WIN, dtype=jnp.int32)
    source = (k % B) * A + k // B
    pick = (source[:, None] == k[None, :]).astype(BF)
    amp = jnp.dot(pick, amplitude, preferred_element_type=F32).astype(BF)
    amp = jnp.dot(amp, pick.T, preferred_element_type=F32).astype(BF)
    region = gather_region(spectrum, rim)
    n_leds = lax.axis_size("ky") * lax.axis_size("kx")
    frame, term = compute(starts, region, pupil_field, amp, n_leds)
    pupil_grad = reduce_terms(term)
    spectrum_grad = scatter_frame(frame, t, rim)
    return (spectrum_grad, pupil_grad)


def solution(mesh):
    return jax.shard_map(
        body,
        mesh=mesh,
        in_specs=(P(None, "ky", "kx"), P(), P("ky", "kx"), P("ky", "kx", None)),
        out_specs=(P(None, "ky", "kx"), P(("ky", "kx"))),
        check_vma=False,
    )
```

time: 622 us -> 261 us (0.42); the launches traced: 613 us -> 260 us
  waiting for transfers between devices: 204 us -> 29.9 us
  local copies, waits for them, and re-layouts: 194 us -> 22.6 us
  matrix products: 86.5 us -> 5.93 us
  Pallas kernels: 0 us -> 56.7 us
  starting transfers between devices: 36 us -> 86.5 us
  other arithmetic: 75.7 us -> 56 us
  between operations: 16.3 us -> 2.38 us
    unnamed x2 -> x0, waiting for transfers between devices: 199 us -> none
    convert_element_type x3 -> x8, local copies, waits for them, and re-layouts: 82.2 us -> 0.31 us  [halve(): lax.dynamic_index_in_dim(x, 1 - bit, dim, keepdims=False).astype(dtype)]
    dot_general x8 -> x1, matrix products: 86.5 us -> 5.93 us  [body(): amp = jnp.dot(amp, pick.T, preferred_element_type=F32).astype(BF)]
    pallas_call x0 -> x1, Pallas kernels: none -> 56.7 us  [compute(): pl.pallas_call(functools.partial(kernel, 1.0 / n_leds), out_shape=(jax.Sh...]
    ppermute x8 -> x22, starting transfers between devices: 36 us -> 86.5 us  [the longest x12 49.4 us: shift(): return lax.ppermute(x, axis, pairs)]
    concatenate x0 -> x2, other arithmetic: none -> 46 us  [the longest x1 44.2 us: gather_region(): return jnp.concatenate([top, mid, bottom], axis=1)]
    dynamic_update_slice x1 -> x0, local copies, waits for them, and re-layouts: 45.7 us -> none  [body(): lax.dynamic_update_slice(frame, jnp.stack([grad_real, grad_imag]), (zero_...]
    another operation x7 -> x0, local copies, waits for them, and re-layouts: 27.5 us -> none  [the longest x2 18 us: transform(): parts = stacked.reshape(split_shape)]
  transfers between devices with their start and end apart: 9 -> 22, of which waited for: 3 -> 9; matrix products, arithmetic and copies ran while one was open for 16% -> 11% of each run, Pallas kernels for 0% -> 0%
where the time goes in v1:
time: 261 us; the launch traced here: 260 us
  starting transfers between devices  86.5 us (33%)
  Pallas kernels  56.7 us (22%)
  other arithmetic  56 us (21%)
  waiting for transfers between devices  29.9 us (11%)
  local copies, waits for them, and re-layouts  22.6 us (9%)
  matrix products  5.93 us (2%)
    pallas_call x1, Pallas kernels, compute(): pl.pallas_call(functools.partial(kernel, 1.0 / n_leds), out_shape=(jax.Sh...  56.7 us
    ppermute x12, starting transfers between devices, shift(): return lax.ppermute(x, axis, pairs)  49.4 us
    concatenate x1, other arithmetic, gather_region(): return jnp.concatenate([top, mid, bottom], axis=1)  44.2 us
    ppermute x10, starting transfers between devices, halve(): got = lax.ppermute(send, axis, [(i, i ^ weight) for i in range(n)])  37.1 us
    ppermute x12, waiting for transfers between devices, shift(): return lax.ppermute(x, axis, pairs)  15.7 us
    ppermute x10, waiting for transfers between devices, halve(): got = lax.ppermute(send, axis, [(i, i ^ weight) for i in range(n)])  14.2 us
    dot_general x1, matrix products, body(): amp = jnp.dot(amp, pick.T, preferred_element_type=F32).astype(BF)  5.93 us
  transfers between devices with their start and end apart: 22, of which 9 were waited for; matrix products, arithmetic and copies ran while one was open for 11% of the time, Pallas kernels for 0%

profile of v1, /device:TPU:0, one launch (start us, length us, event | category | flops | bytes accessed | tf_op | source)
XLA Modules:
  0.0 260.0 jit_solution(4579545487183355277)
XLA Ops:
  2.3 5.0 %collective-permute-start = (bf16[2,512,384]{2,1,0:T(8,128)(2,1)S(1)}, bf16[2,512,384]{2,1,0:T(8,128)(2,1)S(1)}, u32[]{:S(2)}, u32[]{:S(2)}) collective-permute-start(bf16[2,512,384]{2,1,0:T(8,128)(2,1)S(1)} %get-tuple-element.27), channel_id=1, source_target_pairs={{0,1},{1,2},{2,3},{4,5},{5,6},{6,7},{8,9},{9,10},{10,11},{12,13},{... | collective-permute-start | bytes 2359304 | tf_op jit(solution)/shard_map/ppermute | solution.py:263
  11.2 3.9 %collective-permute-start.3 = (bf16[2,384,512]{2,1,0:T(8,128)(2,1)}, bf16[2,384,512]{2,1,0:T(8,128)(2,1)}, u32[]{:S(2)}, u32[]{:S(2)}) collective-permute-start(bf16[2,384,512]{2,1,0:T(8,128)(2,1)} %get-tuple-element.24), channel_id=1, source_target_pairs={{0,4},{4,8},{8,12},{12,16},{16,20},{20,24},{24,28},{1,5},{5,9},{9,... | collective-permute-start | bytes 2359304 | tf_op jit(solution)/shard_map/ppermute | solution.py:263
  15.1 8.9 %collective-permute-done = bf16[2,512,384]{2,1,0:T(8,128)(2,1)S(1)} collective-permute-done((bf16[2,512,384]{2,1,0:T(8,128)(2,1)S(1)}, bf16[2,512,384]{2,1,0:T(8,128)(2,1)S(1)}, u32[]{:S(2)}, u32[]{:S(2)}) %collective-permute-start) | collective-permute-done | bytes 786464 | tf_op jit(solution)/shard_map/ppermute | solution.py:263
  24.9 3.3 %collective-permute-done.1 = bf16[2,512,384]{2,1,0:T(8,128)(2,1)S(1)} collective-permute-done((bf16[2,512,384]{2,1,0:T(8,128)(2,1)S(1)}, bf16[2,512,384]{2,1,0:T(8,128)(2,1)S(1)}, u32[]{:S(2)}, u32[]{:S(2)}) %collective-permute-start.1) | collective-permute-done | bytes 786464 | tf_op jit(solution)/shard_map/ppermute | solution.py:263
  32.2 4.1 %collective-permute-start.2 = (bf16[2,384,768]{2,1,0:T(8,128)(2,1)}, bf16[2,384,768]{2,1,0:T(8,128)(2,1)}, u32[]{:S(2)}, u32[]{:S(2)}) collective-permute-start(bf16[2,384,768]{2,1,0:T(8,128)(2,1)} %get-tuple-element.18), channel_id=1, source_target_pairs={{0,4},{4,8},{8,12},{12,16},{16,20},{20,24},{24,28},{1,5},{5,9},{9,... | collective-permute-start | bytes 3538952 | tf_op jit(solution)/shard_map/ppermute | solution.py:263
  36.3 5.9 %fusion.5.amp = bf16[1024,1024]{1,0:T(8,128)(2,1)} fusion(s32[1024]{0:T(1024)S(1)} %fusion.24, bf16[1024,1024]{1,0:T(8,128)(2,1)S(1)} %copy-done), kind=kOutput, calls=%fused_computation.17 | convolution fusion | flops 4299161600 | bytes 4198400 | tf_op jit(solution)/shard_map/dot_general | solution.py:348
  47.6 44.2 %maximum_maximum_fusion.region = bf16[2,1280,1280]{2,1,0:T(8,128)(2,1)} fusion(bf16[2,384,384]{2,1,0:T(8,128)(2,1)S(1)} %get-tuple-element.23, bf16[2,384,512]{2,1,0:T(8,128)(2,1)} %collective-permute-done.5, bf16[2,384,384]{2,1,0:T(8,128)(2,1)S(1)} %get-tuple-element.22, bf16[2,512,384]{2,1,0:T(8,128)(2,1)S(1)} %copy-done.11, ...), kind=kLoop, calls=%fused_computation | loop fusion | flops 58982400 | bytes 13107200 | tf_op jit(solution)/shard_map/concatenate | solution.py:278
  91.9 56.7 %shard_map.95 = (bf16[2,1280,1280]{2,1,0:T(8,128)(2,1)}, f32[2,1024,1024]{2,1,0:T(8,128)}) custom-call(s32[2]{0:T(128)} %pad_add_fusion.starts, bf16[2,1280,1280]{2,1,0:T(8,128)(2,1)} %maximum_maximum_fusion.region, bf16[2,1024,1024]{2,1,0:T(8,128)(2,1)} %pupil.1, bf16[1024,1024]{1,0:T(8,128)(2,1)} %fusion.5.amp, ...), custom_call_target="tpu_custom_call" | custom-call | flops 12999999488 | bytes 30000000 | tf_op jit(solution)/shard_map/pallas_call | solution.py:238
  148.6 4.3 %fusion.27 = (f32[2,2,2,2,2,32,1024]{6,5,4,3,2,1,0:T(8,128)S(1)}, f32[2,2,2,2,2,32,1024]{6,5,4,3,2,1,0:T(8,128)S(1)}) fusion(f32[2,2,2,2,2,64,1024]{6,5,4,3,2,1,0:T(8,128)} %bitcast.54), kind=kLoop, calls=%fused_computation.64 | loop fusion | bytes 16777216 | tf_op jit(solution)/shard_map/slice | solution.py:333
  156.2 13.5 %collective-permute-start.17 = (f32[2,2,2,2,32,1024]{5,4,2,3,1,0:T(8,128)}, f32[2,2,2,2,32,1024]{5,4,2,3,1,0:T(8,128)}, u32[]{:S(2)}, u32[]{:S(2)}) collective-permute-start(f32[2,2,2,2,32,1024]{5,4,2,3,1,0:T(8,128)} %bitcast.53), channel_id=1, source_target_pairs={{0,4},{4,0},{8,12},{12,8},{16,20},{20,16},{24,28},{28,24},{1,5},{5... | collective-permute-start | bytes 6291464 | tf_op jit(solution)/shard_map/ppermute | solution.py:310
  173.5 6.1 %collective-permute-start.8 = (bf16[2,384,768]{2,1,0:T(8,128)(2,1)}, bf16[2,384,768]{2,1,0:T(8,128)(2,1)}, u32[]{:S(2)}, u32[]{:S(2)}) collective-permute-start(bf16[2,384,768]{2,1,0:T(8,128)(2,1)} %get-tuple-element.14), channel_id=1, source_target_pairs={{0,4},{4,8},{8,12},{12,16},{16,20},{20,24},{24,28},{1,5},{5,9},{9,... | collective-permute-start | bytes 3538952 | tf_op jit(solution)/shard_map/ppermute | solution.py:263
  184.8 17.9 %collective-permute-start.6 = (bf16[2,384,512]{2,1,0:T(8,128)(2,1)S(1)}, bf16[2,384,512]{2,1,0:T(8,128)(2,1)S(1)}, u32[]{:S(2)}, u32[]{:S(2)}) collective-permute-start(bf16[2,384,512]{2,1,0:T(8,128)(2,1)S(1)} %get-tuple-element.8), channel_id=1, source_target_pairs={{0,4},{4,8},{8,12},{12,16},{16,20},{20,24},{24,28},{1,5},{5,9},{9,... | collective-permute-start | bytes 2359304 | tf_op jit(solution)/shard_map/ppermute | solution.py:263
  206.0 4.6 %collective-permute-start.10 = (bf16[2,512,384]{2,1,0:T(8,128)(2,1)S(1)}, bf16[2,512,384]{2,1,0:T(8,128)(2,1)S(1)}, u32[]{:S(2)}, u32[]{:S(2)}) collective-permute-start(bf16[2,512,384]{2,1,0:T(8,128)(2,1)S(1)} %get-tuple-element.16), channel_id=1, source_target_pairs={{0,1},{1,2},{2,3},{4,5},{5,6},{6,7},{8,9},{9,10},{10,11},{12,13},{... | collective-permute-start | bytes 2359304 | tf_op jit(solution)/shard_map/ppermute | solution.py:263
  210.6 2.1 bitcast_add_fusion.1
  212.9 8.7 %collective-permute-start.18 = (bf16[2,2,2,32,1024]{4,3,1,2,0:T(8,128)(2,1)S(1)}, bf16[2,2,2,32,1024]{4,3,1,2,0:T(8,128)(2,1)S(1)}, u32[]{:S(2)}, u32[]{:S(2)}) collective-permute-start(bf16[2,2,2,32,1024]{4,3,1,2,0:T(8,128)(2,1)S(1)} %fusion.11), channel_id=1, source_target_pairs={{0,16},{4,20},{8,24},{12,28},{16,0},{20,4},{24,8},{28,12},{1,17},{... | collective-permute-start | bytes 1572872 | tf_op jit(solution)/shard_map/ppermute | solution.py:310
  223.8 2.2 collective-permute-done.11
  227.2 3.0 %convert_add_fusion = f32[2,512,512]{2,1,0:T(8,128)} fusion(bf16[2,512,384]{2,1,0:T(8,128)(2,1)S(1)} %collective-permute-done.11, bf16[2,512,384]{2,1,0:T(8,128)(2,1)S(1)} %collective-permute-done.10, bf16[2,384,512]{2,1,0:T(8,128)(2,1)S(1)} %collective-permute-done.7, bf16[2,384,512]{2,1,0:T(8,128)(2,1)S(1)} %collective-permute-done.6, ...), kind=kLoop, calls=%fused_computation.13 | loop fusion | flops 4718592 | bytes 6291456 | tf_op jit(solution)/shard_map/add | solution.py:302
  230.2 2.1 collective-permute-done.18
  232.6 4.5 %collective-permute-start.19 = (bf16[2,2,32,1024]{3,2,0,1:T(8,128)(2,1)S(1)}, bf16[2,2,32,1024]{3,2,0,1:T(8,128)(2,1)S(1)}, u32[]{:S(2)}, u32[]{:S(2)}) collective-permute-start(bf16[2,2,32,1024]{3,2,0,1:T(8,128)(2,1)S(1)} %fusion.13), channel_id=1, source_target_pairs={{0,8},{4,12},{8,0},{12,4},{16,24},{20,28},{24,16},{28,20},{1,9},{5... | collective-permute-start | bytes 786440 | tf_op jit(solution)/shard_map/ppermute | solution.py:310
  237.3 6.5 %collective-permute-done.19 = bf16[2,2,32,1024]{3,2,0,1:T(8,128)(2,1)S(1)} collective-permute-done((bf16[2,2,32,1024]{3,2,0,1:T(8,128)(2,1)S(1)}, bf16[2,2,32,1024]{3,2,0,1:T(8,128)(2,1)S(1)}, u32[]{:S(2)}, u32[]{:S(2)}) %collective-permute-start.19) | collective-permute-done | bytes 262176 | tf_op jit(solution)/shard_map/ppermute | solution.py:310
  243.9 2.5 collective-permute-start.20
  248.2 2.6 %collective-permute-done.20 = bf16[2,32,1024]{2,1,0:T(8,128)(2,1)S(1)} collective-permute-done((bf16[2,32,1024]{2,1,0:T(8,128)(2,1)S(1)}, bf16[2,32,1024]{2,1,0:T(8,128)(2,1)S(1)}, u32[]{:S(2)}, u32[]{:S(2)}) %collective-permute-start.20) | collective-permute-done | bytes 131104 | tf_op jit(solution)/shard_map/ppermute | solution.py:310
  250.8 3.1 %collective-permute-start.21 = (bf16[32,1024]{1,0:T(8,128)(2,1)S(1)}, bf16[32,1024]{1,0:T(8,128)(2,1)S(1)}, u32[]{:S(2)}, u32[]{:S(2)}) collective-permute-start(bf16[32,1024]{1,0:T(8,128)(2,1)S(1)} %fusion.17), channel_id=1, source_target_pairs={{0,2},{1,3},{2,0},{3,1},{4,6},{5,7},{6,4},{7,5},{8,10},{9,11},{10,... | collective-permute-start | bytes 196616 | tf_op jit(solution)/shard_map/ppermute | solution.py:310
  254.0 2.3 collective-permute-start.16
  (94 shorter events, 39.4 us)
Async XLA Ops:
  0.6 35.7 %copy-start = (bf16[1024,1024]{1,0:T(8,128)(2,1)S(1)}, bf16[1024,1024]{1,0:T(8,128)(2,1)}, u32[]{:S(2)}) copy-start(bf16[1024,1024]{1,0:T(8,128)(2,1)} %param.10) | copy-start | bytes 6291460
  2.3 21.7 %collective-permute-start = (bf16[2,512,384]{2,1,0:T(8,128)(2,1)S(1)}, bf16[2,512,384]{2,1,0:T(8,128)(2,1)S(1)}, u32[]{:S(2)}, u32[]{:S(2)}) collective-permute-start(bf16[2,512,384]{2,1,0:T(8,128)(2,1)S(1)} %get-tuple-element.27), channel_id=1, source_target_pairs={{0,1},{1,2},{2,3},{4,5},{5,6},{6,7},{8,9},{9,10},{10,11},{12,13},{... | collective-permute-start | bytes 2359304 | tf_op jit(solution)/shard_map/ppermute | solution.py:263
  7.3 20.9 %collective-permute-start.1 = (bf16[2,512,384]{2,1,0:T(8,128)(2,1)S(1)}, bf16[2,512,384]{2,1,0:T(8,128)(2,1)S(1)}, u32[]{:S(2)}, u32[]{:S(2)}) collective-permute-start(bf16[2,512,384]{2,1,0:T(8,128)(2,1)S(1)} %get-tuple-element.26), channel_id=1, source_target_pairs={{1,0},{2,1},{3,2},{5,4},{6,5},{7,6},{9,8},{10,9},{11,10},{13,12},{... | collective-permute-start | bytes 2359304 | tf_op jit(solution)/shard_map/ppermute | solution.py:263
  9.9 37.7 %collective-permute-start.5 = (bf16[2,384,512]{2,1,0:T(8,128)(2,1)}, bf16[2,384,512]{2,1,0:T(8,128)(2,1)}, u32[]{:S(2)}, u32[]{:S(2)}) collective-permute-start(bf16[2,384,512]{2,1,0:T(8,128)(2,1)} %get-tuple-element.25), channel_id=1, source_target_pairs={{4,0},{8,4},{12,8},{16,12},{20,16},{24,20},{28,24},{5,1},{9,5},{13... | collective-permute-start | bytes 2359304 | tf_op jit(solution)/shard_map/ppermute | solution.py:263
  11.2 36.4 %collective-permute-start.3 = (bf16[2,384,512]{2,1,0:T(8,128)(2,1)}, bf16[2,384,512]{2,1,0:T(8,128)(2,1)}, u32[]{:S(2)}, u32[]{:S(2)}) collective-permute-start(bf16[2,384,512]{2,1,0:T(8,128)(2,1)} %get-tuple-element.24), channel_id=1, source_target_pairs={{0,4},{4,8},{8,12},{12,16},{16,20},{20,24},{24,28},{1,5},{5,9},{9,... | collective-permute-start | bytes 2359304 | tf_op jit(solution)/shard_map/ppermute | solution.py:263
  30.9 13.8 %collective-permute-start.4 = (bf16[2,384,768]{2,1,0:T(8,128)(2,1)}, bf16[2,384,768]{2,1,0:T(8,128)(2,1)}, u32[]{:S(2)}, u32[]{:S(2)}) collective-permute-start(bf16[2,384,768]{2,1,0:T(8,128)(2,1)} %get-tuple-element.19), channel_id=1, source_target_pairs={{4,0},{8,4},{12,8},{16,12},{20,16},{24,20},{28,24},{5,1},{9,5},{13... | collective-permute-start | bytes 3538952 | tf_op jit(solution)/shard_map/ppermute | solution.py:263
  32.2 14.0 %collective-permute-start.2 = (bf16[2,384,768]{2,1,0:T(8,128)(2,1)}, bf16[2,384,768]{2,1,0:T(8,128)(2,1)}, u32[]{:S(2)}, u32[]{:S(2)}) collective-permute-start(bf16[2,384,768]{2,1,0:T(8,128)(2,1)} %get-tuple-element.18), channel_id=1, source_target_pairs={{0,4},{4,8},{8,12},{12,16},{16,20},{20,24},{24,28},{1,5},{5,9},{9,... | collective-permute-start | bytes 3538952 | tf_op jit(solution)/shard_map/ppermute | solution.py:263
  152.9 26.7 %copy-start.5 = (f32[2,2,2,2,2,32,1024]{6,5,4,3,2,1,0:T(8,128)}, f32[2,2,2,2,2,32,1024]{6,5,4,3,2,1,0:T(8,128)S(1)}, u32[]{:S(2)}) copy-start(f32[2,2,2,2,2,32,1024]{6,5,4,3,2,1,0:T(8,128)S(1)} %get-tuple-element.6) | copy-start | bytes 12582916
  156.2 49.8 %collective-permute-start.17 = (f32[2,2,2,2,32,1024]{5,4,2,3,1,0:T(8,128)}, f32[2,2,2,2,32,1024]{5,4,2,3,1,0:T(8,128)}, u32[]{:S(2)}, u32[]{:S(2)}) collective-permute-start(f32[2,2,2,2,32,1024]{5,4,2,3,1,0:T(8,128)} %bitcast.53), channel_id=1, source_target_pairs={{0,4},{4,0},{8,12},{12,8},{16,20},{20,16},{24,28},{28,24},{1,5},{5... | collective-permute-start | bytes 6291464 | tf_op jit(solution)/shard_map/ppermute | solution.py:310
  172.2 12.5 %collective-permute-start.9 = (bf16[2,384,768]{2,1,0:T(8,128)(2,1)}, bf16[2,384,768]{2,1,0:T(8,128)(2,1)S(1)}, u32[]{:S(2)}, u32[]{:S(2)}) collective-permute-start(bf16[2,384,768]{2,1,0:T(8,128)(2,1)} %get-tuple-element.15), channel_id=1, source_target_pairs={{4,0},{8,4},{12,8},{16,12},{20,16},{24,20},{28,24},{5,1},{9,5},{13... | collective-permute-start | bytes 3538952 | tf_op jit(solution)/shard_map/ppermute | solution.py:263
  173.5 29.1 %collective-permute-start.8 = (bf16[2,384,768]{2,1,0:T(8,128)(2,1)}, bf16[2,384,768]{2,1,0:T(8,128)(2,1)}, u32[]{:S(2)}, u32[]{:S(2)}) collective-permute-start(bf16[2,384,768]{2,1,0:T(8,128)(2,1)} %get-tuple-element.14), channel_id=1, source_target_pairs={{0,4},{4,8},{8,12},{12,16},{16,20},{20,24},{24,28},{1,5},{5,9},{9,... | collective-permute-start | bytes 3538952 | tf_op jit(solution)/shard_map/ppermute | solution.py:263
  181.1 31.8 %collective-permute-start.12 = (f32[2,2,2,2,32,1024]{5,4,3,2,1,0:T(8,128)}, f32[2,2,2,2,32,1024]{5,4,3,2,1,0:T(8,128)}, u32[]{:S(2)}, u32[]{:S(2)}) collective-permute-start(f32[2,2,2,2,32,1024]{5,4,3,2,1,0:T(8,128)} %dynamic-slice_bitcast_fusion), channel_id=1, source_target_pairs={{0,4},{4,0},{8,12},{12,8},{16,20},{20,16},{24,28},{28,24},{1,5},{5... | collective-permute-start | bytes 6291464 | tf_op jit(solution)/shard_map/ppermute | solution.py:310
  183.4 40.2 %collective-permute-start.7 = (bf16[2,384,512]{2,1,0:T(8,128)(2,1)S(1)}, bf16[2,384,512]{2,1,0:T(8,128)(2,1)S(1)}, u32[]{:S(2)}, u32[]{:S(2)}) collective-permute-start(bf16[2,384,512]{2,1,0:T(8,128)(2,1)S(1)} %get-tuple-element.9), channel_id=1, source_target_pairs={{4,0},{8,4},{12,8},{16,12},{20,16},{24,20},{28,24},{5,1},{9,5},{13... | collective-permute-start | bytes 2359304 | tf_op jit(solution)/shard_map/ppermute | solution.py:263
  184.8 39.0 %collective-permute-start.6 = (bf16[2,384,512]{2,1,0:T(8,128)(2,1)S(1)}, bf16[2,384,512]{2,1,0:T(8,128)(2,1)S(1)}, u32[]{:S(2)}, u32[]{:S(2)}) collective-permute-start(bf16[2,384,512]{2,1,0:T(8,128)(2,1)S(1)} %get-tuple-element.8), channel_id=1, source_target_pairs={{0,4},{4,8},{8,12},{12,16},{16,20},{20,24},{24,28},{1,5},{5,9},{9,... | collective-permute-start | bytes 2359304 | tf_op jit(solution)/shard_map/ppermute | solution.py:263
  204.6 21.4 %collective-permute-start.11 = (bf16[2,512,384]{2,1,0:T(8,128)(2,1)S(1)}, bf16[2,512,384]{2,1,0:T(8,128)(2,1)S(1)}, u32[]{:S(2)}, u32[]{:S(2)}) collective-permute-start(bf16[2,512,384]{2,1,0:T(8,128)(2,1)S(1)} %get-tuple-element.17), channel_id=1, source_target_pairs={{1,0},{2,1},{3,2},{5,4},{6,5},{7,6},{9,8},{10,9},{11,10},{13,12},{... | collective-permute-start | bytes 2359304 | tf_op jit(solution)/shard_map/ppermute | solution.py:263
  206.0 21.2 %collective-permute-start.10 = (bf16[2,512,384]{2,1,0:T(8,128)(2,1)S(1)}, bf16[2,512,384]{2,1,0:T(8,128)(2,1)S(1)}, u32[]{:S(2)}, u32[]{:S(2)}) collective-permute-start(bf16[2,512,384]{2,1,0:T(8,128)(2,1)S(1)} %get-tuple-element.16), channel_id=1, source_target_pairs={{0,1},{1,2},{2,3},{4,5},{5,6},{6,7},{8,9},{9,10},{10,11},{12,13},{... | collective-permute-start | bytes 2359304 | tf_op jit(solution)/shard_map/ppermute | solution.py:263
  212.9 19.5 %collective-permute-start.18 = (bf16[2,2,2,32,1024]{4,3,1,2,0:T(8,128)(2,1)S(1)}, bf16[2,2,2,32,1024]{4,3,1,2,0:T(8,128)(2,1)S(1)}, u32[]{:S(2)}, u32[]{:S(2)}) collective-permute-start(bf16[2,2,2,32,1024]{4,3,1,2,0:T(8,128)(2,1)S(1)} %fusion.11), channel_id=1, source_target_pairs={{0,16},{4,20},{8,24},{12,28},{16,0},{20,4},{24,8},{28,12},{1,17},{... | collective-permute-start | bytes 1572872 | tf_op jit(solution)/shard_map/ppermute | solution.py:310
  223.7 13.4 %collective-permute-start.13 = (bf16[2,2,2,32,1024]{4,3,2,1,0:T(8,128)(2,1)S(1)}, bf16[2,2,2,32,1024]{4,3,2,1,0:T(8,128)(2,1)S(1)}, u32[]{:S(2)}, u32[]{:S(2)}) collective-permute-start(bf16[2,2,2,32,1024]{4,3,2,1,0:T(8,128)(2,1)S(1)} %fusion.10), channel_id=1, source_target_pairs={{0,8},{4,12},{8,0},{12,4},{16,24},{20,28},{24,16},{28,20},{1,9},{5... | collective-permute-start | bytes 1572872 | tf_op jit(solution)/shard_map/ppermute | solution.py:310
  232.6 11.2 %collective-permute-start.19 = (bf16[2,2,32,1024]{3,2,0,1:T(8,128)(2,1)S(1)}, bf16[2,2,32,1024]{3,2,0,1:T(8,128)(2,1)S(1)}, u32[]{:S(2)}, u32[]{:S(2)}) collective-permute-start(bf16[2,2,32,1024]{3,2,0,1:T(8,128)(2,1)S(1)} %fusion.13), channel_id=1, source_target_pairs={{0,8},{4,12},{8,0},{12,4},{16,24},{20,28},{24,16},{28,20},{1,9},{5... | collective-permute-start | bytes 786440 | tf_op jit(solution)/shard_map/ppermute | solution.py:310
  237.2 9.2 %collective-permute-start.14 = (bf16[2,2,32,1024]{3,2,1,0:T(8,128)(2,1)S(1)}, bf16[2,2,32,1024]{3,2,1,0:T(8,128)(2,1)S(1)}, u32[]{:S(2)}, u32[]{:S(2)}) collective-permute-start(bf16[2,2,32,1024]{3,2,1,0:T(8,128)(2,1)S(1)} %fusion.12), channel_id=1, source_target_pairs={{0,16},{4,20},{8,24},{12,28},{16,0},{20,4},{24,8},{28,12},{1,17},{... | collective-permute-start | bytes 786440 | tf_op jit(solution)/shard_map/ppermute | solution.py:310
  243.9 6.9 %collective-permute-start.20 = (bf16[2,32,1024]{2,1,0:T(8,128)(2,1)S(1)}, bf16[2,32,1024]{2,1,0:T(8,128)(2,1)S(1)}, u32[]{:S(2)}, u32[]{:S(2)}) collective-permute-start(bf16[2,32,1024]{2,1,0:T(8,128)(2,1)S(1)} %fusion.15), channel_id=1, source_target_pairs={{0,1},{1,0},{2,3},{3,2},{4,5},{5,4},{6,7},{7,6},{8,9},{9,8},{10,11... | collective-permute-start | bytes 393224 | tf_op jit(solution)/shard_map/ppermute | solution.py:310
  246.6 7.4 %collective-permute-start.15 = (bf16[2,32,1024]{2,1,0:T(8,128)(2,1)S(1)}, bf16[2,32,1024]{2,1,0:T(8,128)(2,1)S(1)}, u32[]{:S(2)}, u32[]{:S(2)}) collective-permute-start(bf16[2,32,1024]{2,1,0:T(8,128)(2,1)S(1)} %fusion.14), channel_id=1, source_target_pairs={{0,1},{1,0},{2,3},{3,2},{4,5},{5,4},{6,7},{7,6},{8,9},{9,8},{10,11... | collective-permute-start | bytes 393224 | tf_op jit(solution)/shard_map/ppermute | solution.py:310
  250.8 7.4 %collective-permute-start.21 = (bf16[32,1024]{1,0:T(8,128)(2,1)S(1)}, bf16[32,1024]{1,0:T(8,128)(2,1)S(1)}, u32[]{:S(2)}, u32[]{:S(2)}) collective-permute-start(bf16[32,1024]{1,0:T(8,128)(2,1)S(1)} %fusion.17), channel_id=1, source_target_pairs={{0,2},{1,3},{2,0},{3,1},{4,6},{5,7},{6,4},{7,5},{8,10},{9,11},{10,... | collective-permute-start | bytes 196616 | tf_op jit(solution)/shard_map/ppermute | solution.py:310
  254.0 5.2 %collective-permute-start.16 = (bf16[32,1024]{1,0:T(8,128)(2,1)S(1)}, bf16[32,1024]{1,0:T(8,128)(2,1)S(1)}, u32[]{:S(2)}, u32[]{:S(2)}) collective-permute-start(bf16[32,1024]{1,0:T(8,128)(2,1)S(1)} %fusion.16), channel_id=1, source_target_pairs={{0,2},{1,3},{2,0},{3,1},{4,6},{5,7},{6,4},{7,5},{8,10},{9,11},{10,... | collective-permute-start | bytes 196616 | tf_op jit(solution)/shard_map/ppermute | solution.py:310
  (13 other events, 112.9 us)

commit v2 on v1

--- a/solution.py
+++ b/solution.py
@@ -257,25 +257,116 @@
     )(starts, region, pupil, amp, jnp.asarray(lane), jnp.asarray(rows), jnp.asarray(tw), jnp.asarray(tw_rows))
 
 
+MESH = pl.DeviceIdType.MESH
+
+
+def remote(src, dst, send, recv, where):
+    return pltpu.make_async_remote_copy(
+        src_ref=src, dst_ref=dst, send_sem=send, recv_sem=recv, device_id=where, device_id_type=MESH
+    )
+
+
+def greet(sides):
+    barrier = pltpu.get_barrier_semaphore()
+    count = jnp.int32(0)
+    for cond, where in sides:
+        @pl.when(cond)
+        def _(where=where):
+            pl.semaphore_signal(barrier, inc=1, device_id=where, device_id_type=MESH)
+        count = count + jnp.where(cond, 1, 0)
+    pl.semaphore_wait(barrier, count)
+
+
+def halo_kernel(n_ky, n_kx, rim, tile, region, send, recv):
+    t = tile.shape[1]
+    ky, kx = lax.axis_index("ky"), lax.axis_index("kx")
+    has = {"u": ky > 0, "d": ky < n_ky - 1, "l": kx > 0, "r": kx < n_kx - 1}
+    dev = {"u": (ky - 1, kx), "d": (ky + 1, kx), "l": (ky, kx - 1), "r": (ky, kx + 1)}
+    back = {"u": "d", "d": "u", "l": "r", "r": "l"}
+    far = {"u": pl.ds(0, rim), "d": pl.ds(rim + t, rim), "l": pl.ds(0, rim), "r": pl.ds(rim + t, rim), "": pl.ds(rim, t)}
+    near = {"u": pl.ds(0, rim), "l": pl.ds(0, rim), "d": pl.ds(t - rim, rim), "r": pl.ds(t - rim, rim)}
+    greet([(has[k], dev[k]) for k in "udlr"])
+    whole = pl.ds(0, t)
+
+    def strip(q, k):
+        i = q * 8 + "udlr".index(k)
+        rows = near[k] if k in "ud" else whole
+        cols = near[k] if k in "lr" else whole
+        o = back[k]
+        dst = region.at[q, far[o] if k in "ud" else far[""], far[o] if k in "lr" else far[""]]
+        return remote(tile.at[q, rows, cols], dst, send.at[i], recv.at[i], dev[k])
+
+    def corner(q, k, side):
+        i = q * 8 + 4 + "ud".index(k) * 2 + "lr".index(side)
+        rows = pl.ds(rim, rim) if k == "u" else pl.ds(t, rim)
+        return remote(
+            region.at[q, rows, far[side]], region.at[q, far[back[k]], far[side]], send.at[i], recv.at[i], dev[k]
+        )
+
+    for q in range(2):
+        for k in "lrud":
+            @pl.when(has[k])
+            def _(q=q, k=k):
+                strip(q, k).start()
+    for q in range(2):
+        region[q, rim : rim + t, rim : rim + t] = tile[q]
+    for k in "udlr":
+        @pl.when(jnp.logical_not(has[k]))
+        def _(k=k):
+            for q in range(2):
+                if k in "ud":
+                    region[q, far[k], :] = jnp.zeros((rim, region.shape[2]), region.dtype)
+                else:
+                    region[q, far[""], far[k]] = jnp.zeros((t, rim), region.dtype)
+                    for v in "ud":
+                        @pl.when(has[v])
+                        def _(q=q, k=k, v=v):
+                            region[q, far[v], far[k]] = jnp.zeros((rim, rim), region.dtype)
+    for q in range(2):
+        for side in "lr":
+            @pl.when(has[side])
+            def _(q=q, side=side):
+                strip(q, back[side]).wait_recv()
+                for k in "ud":
+                    @pl.when(has[k])
+                    def _(k=k):
+                        corner(q, k, side).start()
+    for q in range(2):
+        for k in "ud":
+            @pl.when(has[k])
+            def _(q=q, k=k):
+                strip(q, back[k]).wait_recv()
+                for side in "lr":
+                    @pl.when(has[side])
+                    def _(side=side):
+                        corner(q, back[k], side).wait_recv()
+                        corner(q, k, side).wait_send()
+        for k in "udlr":
+            @pl.when(has[k])
+            def _(q=q, k=k):
+                strip(q, k).wait_send()
+
+
+def gather_region(tile, rim):
+    t = tile.shape[1]
+    side = t + 2 * rim
+    vm = pl.BlockSpec(memory_space=pltpu.VMEM)
+    return pl.pallas_call(
+        functools.partial(halo_kernel, lax.axis_size("ky"), lax.axis_size("kx"), rim),
+        out_shape=jax.ShapeDtypeStruct((2, side, side), tile.dtype),
+        in_specs=[vm],
+        out_specs=vm,
+        scratch_shapes=[pltpu.SemaphoreType.DMA((16,)), pltpu.SemaphoreType.DMA((16,))],
+        compiler_params=pltpu.CompilerParams(
+            collective_id=0, has_side_effects=True, vmem_limit_bytes=32 * 1024 * 1024
+        ),
+    )(tile)
+
+
 def shift(x, axis, step):
     n = lax.axis_size(axis)
     pairs = [(i, i + step) for i in range(n) if 0 <= i + step < n]
     return lax.ppermute(x, axis, pairs)
-
-
-def gather_region(tile, rim):
-    t = tile.shape[1]
-    left = shift(tile[:, :, t - rim :], "kx", 1)
-    right = shift(tile[:, :, :rim], "kx", -1)
-    up = shift(tile[:, t - rim :, :], "ky", 1)
-    down = shift(tile[:, :rim, :], "ky", -1)
-    sides = jnp.concatenate([left, right], axis=2)
-    up_s = shift(sides[:, t - rim :, :], "ky", 1)
-    down_s = shift(sides[:, :rim, :], "ky", -1)
-    top = jnp.concatenate([up_s[:, :, :rim], up, up_s[:, :, rim:]], axis=2)
-    mid = jnp.concatenate([left, tile, right], axis=2)
-    bottom = jnp.concatenate([down_s[:, :, :rim], down, down_s[:, :, rim:]], axis=2)
-    return jnp.concatenate([top, mid, bottom], axis=1)
 
 
 def fold_rows(mid, from_up, from_down, rim):

time: 261 us -> 221 us (0.85)
  other arithmetic: 56 us -> 12.2 us
  Pallas kernels: 56.7 us -> 80.3 us
  waiting for transfers between devices: 29.9 us -> 17.5 us
  starting transfers between devices: 86.5 us -> 77.4 us
    concatenate x1 -> x0, other arithmetic: 44.2 us -> none  [gather_region(): return jnp.concatenate([top, mid, bottom], axis=1)]
    pallas_call x0 -> x1, Pallas kernels: none -> 23.8 us  [gather_region(): pl.pallas_call(functools.partial(halo_kernel, lax.axis_size('ky'), lax.ax...]
    ppermute x12 -> x6, waiting for transfers between devices: 15.7 us -> 5.19 us  [shift(): return lax.ppermute(x, axis, pairs)]
    slice x5 -> x0, local copies, waits for them, and re-layouts: 7.38 us -> none  [the longest x1 1.69 us: gather_region(): right = shift(tile[:, :, :rim], 'kx', -1)]
    ppermute x12 -> x6, starting transfers between devices: 49.4 us -> 43.9 us  [shift(): return lax.ppermute(x, axis, pairs)]
    slice x1, local copies, waits for them, and re-layouts: 4.32 us -> 8.43 us  [reduce_terms(): first = chain(flat[..., :half, :], core + y_bits + x_bits)]
    ppermute x10, starting transfers between devices: 37.1 us -> 33.5 us  [halve(): got = lax.ppermute(send, axis, [(i, i ^ weight) for i in range(n)])]
    dynamic_slice x1, local copies, waits for them, and re-layouts: 1.64 us -> 4.28 us  [halve(): keep = lax.dynamic_index_in_dim(x, bit, dim, keepdims=False)]
  transfers between devices with their start and end apart: 22 -> 16, of which waited for: 9 -> 6; matrix products, arithmetic and copies ran while one was open for 11% -> 7% of each run, Pallas kernels for 0% -> 0%
where the time goes in v2:
time: 221 us; the launch traced here: 220 us
  Pallas kernels  80.3 us (36%)
  starting transfers between devices  77.4 us (35%)
  local copies, waits for them, and re-layouts  24.6 us (11%)
  waiting for transfers between devices  17.5 us (8%)
  other arithmetic  12.2 us (6%)
  matrix products  5.93 us (3%)
  between operations  2.41 us (1%)
    pallas_call x1, Pallas kernels, compute(): pl.pallas_call(functools.partial(kernel, 1.0 / n_leds), out_shape=(jax.Sh...  56.5 us
    ppermute x6, starting transfers between devices, shift(): return lax.ppermute(x, axis, pairs)  43.9 us
    ppermute x10, starting transfers between devices, halve(): got = lax.ppermute(send, axis, [(i, i ^ weight) for i in range(n)])  33.5 us
    pallas_call x1, Pallas kernels, gather_region(): pl.pallas_call(functools.partial(halo_kernel, lax.axis_size('ky'), lax.ax...  23.8 us
    ppermute x10, waiting for transfers between devices, halve(): got = lax.ppermute(send, axis, [(i, i ^ weight) for i in range(n)])  12.3 us
    slice x1, local copies, waits for them, and re-layouts, reduce_terms(): first = chain(flat[..., :half, :], core + y_bits + x_bits)  8.43 us
    dot_general x1, matrix products, body(): amp = jnp.dot(amp, pick.T, preferred_element_type=F32).astype(BF)  5.93 us
    unnamed x21, local copies, waits for them, and re-layouts  5.25 us
  transfers between devices with their start and end apart: 16, of which 6 were waited for; matrix products, arithmetic and copies ran while one was open for 7% of the time, Pallas kernels for 0%

profile of v2, /device:TPU:0, one launch (start us, length us, event | category | flops | bytes accessed | tf_op | source)
XLA Modules:
  0.0 220.4 jit_solution(9386663703479313344)
XLA Ops:
  3.3 23.8 %shard_map.95.region = bf16[2,1280,1280]{2,1,0:T(8,128)(2,1)S(1)} custom-call(bf16[2,512,512]{2,1,0:T(8,128)(2,1)S(1)} %copy-done.3), custom_call_target="tpu_custom_call" | custom-call | tf_op jit(solution)/shard_map/pallas_call | solution.py:354
  27.1 2.7 %copy-done.2 = bf16[2,1280,1280]{2,1,0:T(8,128)(2,1)} copy-done((bf16[2,1280,1280]{2,1,0:T(8,128)(2,1)}, bf16[2,1280,1280]{2,1,0:T(8,128)(2,1)S(1)}, u32[]{:S(2)}) %copy-start.2) | copy-done | bytes 6553624
  31.7 5.9 %fusion.5.amp = bf16[1024,1024]{1,0:T(8,128)(2,1)} fusion(s32[1024]{0:T(1024)S(1)} %fusion.24, bf16[1024,1024]{1,0:T(8,128)(2,1)S(1)} %copy-done), kind=kOutput, calls=%fused_computation.16 | convolution fusion | flops 4299161600 | bytes 4198400 | tf_op jit(solution)/shard_map/dot_general | solution.py:439
  37.7 56.5 %shard_map.96 = (bf16[2,1280,1280]{2,1,0:T(8,128)(2,1)}, f32[2,1024,1024]{2,1,0:T(8,128)}) custom-call(s32[2]{0:T(128)} %pad_add_fusion.starts, bf16[2,1280,1280]{2,1,0:T(8,128)(2,1)} %copy-done.2, bf16[2,1024,1024]{2,1,0:T(8,128)(2,1)} %pupil.1, bf16[1024,1024]{1,0:T(8,128)(2,1)} %fusion.5.amp, bf16[2,768,256]{2,1,0:T(8,128)(2,1)} %constant.207.clone.lane_t, ...), custom_call_target="tpu_custom_call" | custom-call | flops 12999999488 | bytes 30000000 | tf_op jit(solution)/shard_map/pallas_call | solution.py:238
  94.2 8.4 %fusion.27 = (f32[2,2,2,2,2,32,1024]{6,5,4,3,2,1,0:T(8,128)}, f32[2,2,2,2,2,32,1024]{6,5,4,3,2,1,0:T(8,128)}) fusion(f32[2,2,2,2,2,64,1024]{6,5,4,3,2,1,0:T(8,128)} %bitcast.54), kind=kLoop, calls=%fused_computation.61 | loop fusion | bytes 16777216 | tf_op jit(solution)/shard_map/slice | solution.py:424
  102.6 4.3 %constant_dynamic-slice_fusion.1 = (f32[2,2,1,2,2,32,1024]{6,5,4,3,2,1,0:T(8,128)}, f32[2,2,1,2,2,32,1024]{6,5,4,3,2,1,0:T(8,128)S(1)}) fusion(f32[2,2,2,2,2,32,1024]{6,5,4,3,2,1,0:T(8,128)} %get-tuple-element.7, s32[]{:T(128)S(6)} %select_n.122, s32[]{:T(128)S(6)} %select_n.123), kind=kLoop, calls=%fused_computation.54 | loop fusion | bytes 8388616 | tf_op jit(solution)/shard_map/jit(dynamic_index_in_dim)/dynamic_slice | solution.py:399
  108.5 11.2 %collective-permute-start.11 = (f32[2,2,2,2,32,1024]{5,4,2,3,1,0:T(8,128)}, f32[2,2,2,2,32,1024]{5,4,2,3,1,0:T(8,128)}, u32[]{:S(2)}, u32[]{:S(2)}) collective-permute-start(f32[2,2,2,2,32,1024]{5,4,2,3,1,0:T(8,128)} %bitcast.53), channel_id=1, source_target_pairs={{0,4},{4,0},{8,12},{12,8},{16,20},{20,16},{24,28},{28,24},{1,5},{5... | collective-permute-start | bytes 6291464 | tf_op jit(solution)/shard_map/ppermute | solution.py:401
  123.7 4.1 %collective-permute-start.2 = (bf16[2,384,768]{2,1,0:T(8,128)(2,1)}, bf16[2,384,768]{2,1,0:T(8,128)(2,1)}, u32[]{:S(2)}, u32[]{:S(2)}) collective-permute-start(bf16[2,384,768]{2,1,0:T(8,128)(2,1)} %get-tuple-element.14), channel_id=1, source_target_pairs={{0,4},{4,8},{8,12},{12,16},{16,20},{20,24},{24,28},{1,5},{5,9},{9,... | collective-permute-start | bytes 3538952 | tf_op jit(solution)/shard_map/ppermute | solution.py:369
  132.2 18.9 %collective-permute-start = (bf16[2,384,512]{2,1,0:T(8,128)(2,1)}, bf16[2,384,512]{2,1,0:T(8,128)(2,1)S(1)}, u32[]{:S(2)}, u32[]{:S(2)}) collective-permute-start(bf16[2,384,512]{2,1,0:T(8,128)(2,1)} %get-tuple-element.8), channel_id=1, source_target_pairs={{0,4},{4,8},{8,12},{12,16},{16,20},{20,24},{24,28},{1,5},{5,9},{9,... | collective-permute-start | bytes 2359304 | tf_op jit(solution)/shard_map/ppermute | solution.py:369
  151.1 2.0 add_convert_fusion
  154.7 16.8 %collective-permute-start.4 = (bf16[2,512,384]{2,1,0:T(8,128)(2,1)S(1)}, bf16[2,512,384]{2,1,0:T(8,128)(2,1)S(1)}, u32[]{:S(2)}, u32[]{:S(2)}) collective-permute-start(bf16[2,512,384]{2,1,0:T(8,128)(2,1)S(1)} %get-tuple-element.16), channel_id=1, source_target_pairs={{0,1},{1,2},{2,3},{4,5},{5,6},{6,7},{8,9},{9,10},{10,11},{12,13},{... | collective-permute-start | bytes 2359304 | tf_op jit(solution)/shard_map/ppermute | solution.py:369
  171.5 2.1 bitcast_add_fusion.1
  173.8 7.3 %collective-permute-start.12 = (bf16[2,2,2,32,1024]{4,3,1,2,0:T(8,128)(2,1)S(1)}, bf16[2,2,2,32,1024]{4,3,1,2,0:T(8,128)(2,1)S(1)}, u32[]{:S(2)}, u32[]{:S(2)}) collective-permute-start(bf16[2,2,2,32,1024]{4,3,1,2,0:T(8,128)(2,1)S(1)} %fusion.11), channel_id=1, source_target_pairs={{0,16},{4,20},{8,24},{12,28},{16,0},{20,4},{24,8},{28,12},{1,17},{... | collective-permute-start | bytes 1572872 | tf_op jit(solution)/shard_map/ppermute | solution.py:401
  181.0 2.0 bitcast_add_fusion
  183.2 4.0 %collective-permute-done.5 = bf16[2,512,384]{2,1,0:T(8,128)(2,1)S(1)} collective-permute-done((bf16[2,512,384]{2,1,0:T(8,128)(2,1)S(1)}, bf16[2,512,384]{2,1,0:T(8,128)(2,1)S(1)}, u32[]{:S(2)}, u32[]{:S(2)}) %collective-permute-start.5) | collective-permute-done | bytes 786464 | tf_op jit(solution)/shard_map/ppermute | solution.py:369
  188.4 3.3 %convert_add_fusion = f32[2,512,512]{2,1,0:T(8,128)} fusion(bf16[2,512,384]{2,1,0:T(8,128)(2,1)S(1)} %collective-permute-done.5, bf16[2,512,384]{2,1,0:T(8,128)(2,1)S(1)} %collective-permute-done.4, bf16[2,384,512]{2,1,0:T(8,128)(2,1)} %collective-permute-done.1, bf16[2,384,512]{2,1,0:T(8,128)(2,1)S(1)} %collective-permute-done, ...), kind=kLoop, calls=%fused_computation.12 | loop fusion | flops 4718592 | bytes 6291456 | tf_op jit(solution)/shard_map/add | solution.py:393
  191.9 4.9 %collective-permute-start.13 = (bf16[2,2,32,1024]{3,2,0,1:T(8,128)(2,1)S(1)}, bf16[2,2,32,1024]{3,2,0,1:T(8,128)(2,1)S(1)}, u32[]{:S(2)}, u32[]{:S(2)}) collective-permute-start(bf16[2,2,32,1024]{3,2,0,1:T(8,128)(2,1)S(1)} %fusion.13), channel_id=1, source_target_pairs={{0,8},{4,12},{8,0},{12,4},{16,24},{20,28},{24,16},{28,20},{1,9},{5... | collective-permute-start | bytes 786440 | tf_op jit(solution)/shard_map/ppermute | solution.py:401
  197.1 6.6 %collective-permute-done.13 = bf16[2,2,32,1024]{3,2,0,1:T(8,128)(2,1)S(1)} collective-permute-done((bf16[2,2,32,1024]{3,2,0,1:T(8,128)(2,1)S(1)}, bf16[2,2,32,1024]{3,2,0,1:T(8,128)(2,1)S(1)}, u32[]{:S(2)}, u32[]{:S(2)}) %collective-permute-start.13) | collective-permute-done | bytes 262176 | tf_op jit(solution)/shard_map/ppermute | solution.py:401
  203.9 2.5 %collective-permute-start.14 = (bf16[2,32,1024]{2,1,0:T(8,128)(2,1)S(1)}, bf16[2,32,1024]{2,1,0:T(8,128)(2,1)S(1)}, u32[]{:S(2)}, u32[]{:S(2)}) collective-permute-start(bf16[2,32,1024]{2,1,0:T(8,128)(2,1)S(1)} %fusion.15), channel_id=1, source_target_pairs={{0,1},{1,0},{2,3},{3,2},{4,5},{5,4},{6,7},{7,6},{8,9},{9,8},{10,11... | collective-permute-start | bytes 393224 | tf_op jit(solution)/shard_map/ppermute | solution.py:401
  206.5 1.6 collective-permute-start.9
  208.2 2.6 %collective-permute-done.14 = bf16[2,32,1024]{2,1,0:T(8,128)(2,1)S(1)} collective-permute-done((bf16[2,32,1024]{2,1,0:T(8,128)(2,1)S(1)}, bf16[2,32,1024]{2,1,0:T(8,128)(2,1)S(1)}, u32[]{:S(2)}, u32[]{:S(2)}) %collective-permute-start.14) | collective-permute-done | bytes 131104 | tf_op jit(solution)/shard_map/ppermute | solution.py:401
  210.8 3.5 %collective-permute-start.15 = (bf16[32,1024]{1,0:T(8,128)(2,1)S(1)}, bf16[32,1024]{1,0:T(8,128)(2,1)S(1)}, u32[]{:S(2)}, u32[]{:S(2)}) collective-permute-start(bf16[32,1024]{1,0:T(8,128)(2,1)S(1)} %fusion.17), channel_id=1, source_target_pairs={{0,2},{1,3},{2,0},{3,1},{4,6},{5,7},{6,4},{7,5},{8,10},{9,11},{10,... | collective-permute-start | bytes 196616 | tf_op jit(solution)/shard_map/ppermute | solution.py:401
  214.4 2.1 collective-permute-start.10
  216.5 1.9 collective-permute-done.15
  (65 shorter events, 18.9 us)
Async XLA Ops:
  0.6 31.1 %copy-start = (bf16[1024,1024]{1,0:T(8,128)(2,1)S(1)}, bf16[1024,1024]{1,0:T(8,128)(2,1)}, u32[]{:S(2)}) copy-start(bf16[1024,1024]{1,0:T(8,128)(2,1)} %param.10) | copy-start | bytes 6291460
  27.1 2.7 %copy-start.2 = (bf16[2,1280,1280]{2,1,0:T(8,128)(2,1)}, bf16[2,1280,1280]{2,1,0:T(8,128)(2,1)S(1)}, u32[]{:S(2)}) copy-start(bf16[2,1280,1280]{2,1,0:T(8,128)(2,1)S(1)} %shard_map.95.region) | copy-start | bytes 19660804
  102.6 17.1 %slice-start = ((s8[6553600]{0:T(1024)(128)(4,1)}), s8[4194304]{0:T(1024)(128)(4,1)S(1)}, s32[]{:S(2)}) async-start(s8[6553600]{0:T(1024)(128)(4,1)} %bitcast.55), calls=%async_computation | async-start | bytes 8388608
  102.6 17.1 %slice-start.1 = ((s8[6553600]{0:T(1024)(128)(4,1)}), s8[2359296]{0:T(1024)(128)(4,1)S(1)}, s32[]{:S(2)}) async-start(s8[6553600]{0:T(1024)(128)(4,1)} %bitcast.55), calls=%async_computation.1 | async-start | bytes 4718592
  108.5 46.2 %collective-permute-start.11 = (f32[2,2,2,2,32,1024]{5,4,2,3,1,0:T(8,128)}, f32[2,2,2,2,32,1024]{5,4,2,3,1,0:T(8,128)}, u32[]{:S(2)}, u32[]{:S(2)}) collective-permute-start(f32[2,2,2,2,32,1024]{5,4,2,3,1,0:T(8,128)} %bitcast.53), channel_id=1, source_target_pairs={{0,4},{4,0},{8,12},{12,8},{16,20},{20,16},{24,28},{28,24},{1,5},{5... | collective-permute-start | bytes 6291464 | tf_op jit(solution)/shard_map/ppermute | solution.py:401
  120.1 7.7 %copy-start.5 = (f32[2,2,2,2,2,32,1024]{6,5,4,3,2,1,0:T(8,128)S(1)}, f32[2,2,2,2,2,32,1024]{6,5,4,3,2,1,0:T(8,128)}, u32[]{:S(2)}) copy-start(f32[2,2,2,2,2,32,1024]{6,5,4,3,2,1,0:T(8,128)} %get-tuple-element.6) | copy-start | bytes 12582916
  122.3 9.9 %collective-permute-start.3 = (bf16[2,384,768]{2,1,0:T(8,128)(2,1)}, bf16[2,384,768]{2,1,0:T(8,128)(2,1)S(1)}, u32[]{:S(2)}, u32[]{:S(2)}) collective-permute-start(bf16[2,384,768]{2,1,0:T(8,128)(2,1)} %get-tuple-element.15), channel_id=1, source_target_pairs={{4,0},{8,4},{12,8},{16,12},{20,16},{24,20},{28,24},{5,1},{9,5},{13... | collective-permute-start | bytes 3538952 | tf_op jit(solution)/shard_map/ppermute | solution.py:369
  123.7 27.4 %collective-permute-start.2 = (bf16[2,384,768]{2,1,0:T(8,128)(2,1)}, bf16[2,384,768]{2,1,0:T(8,128)(2,1)}, u32[]{:S(2)}, u32[]{:S(2)}) collective-permute-start(bf16[2,384,768]{2,1,0:T(8,128)(2,1)} %get-tuple-element.14), channel_id=1, source_target_pairs={{0,4},{4,8},{8,12},{12,16},{16,20},{20,24},{24,28},{1,5},{5,9},{9,... | collective-permute-start | bytes 3538952 | tf_op jit(solution)/shard_map/ppermute | solution.py:369
  129.3 44.4 %collective-permute-start.6 = (f32[2,2,2,2,32,1024]{5,4,3,2,1,0:T(8,128)}, f32[2,2,2,2,32,1024]{5,4,3,2,1,0:T(8,128)}, u32[]{:S(2)}, u32[]{:S(2)}) collective-permute-start(f32[2,2,2,2,32,1024]{5,4,3,2,1,0:T(8,128)} %dynamic-slice_bitcast_fusion), channel_id=1, source_target_pairs={{0,4},{4,0},{8,12},{12,8},{16,20},{20,16},{24,28},{28,24},{1,5},{5... | collective-permute-start | bytes 6291464 | tf_op jit(solution)/shard_map/ppermute | solution.py:401
  130.8 52.3 %collective-permute-start.1 = (bf16[2,384,512]{2,1,0:T(8,128)(2,1)}, bf16[2,384,512]{2,1,0:T(8,128)(2,1)}, u32[]{:S(2)}, u32[]{:S(2)}) collective-permute-start(bf16[2,384,512]{2,1,0:T(8,128)(2,1)} %get-tuple-element.9), channel_id=1, source_target_pairs={{4,0},{8,4},{12,8},{16,12},{20,16},{24,20},{28,24},{5,1},{9,5},{13... | collective-permute-start | bytes 2359304 | tf_op jit(solution)/shard_map/ppermute | solution.py:369
  132.2 51.0 %collective-permute-start = (bf16[2,384,512]{2,1,0:T(8,128)(2,1)}, bf16[2,384,512]{2,1,0:T(8,128)(2,1)S(1)}, u32[]{:S(2)}, u32[]{:S(2)}) collective-permute-start(bf16[2,384,512]{2,1,0:T(8,128)(2,1)} %get-tuple-element.8), channel_id=1, source_target_pairs={{0,4},{4,8},{8,12},{12,16},{16,20},{20,24},{24,28},{1,5},{5,9},{9,... | collective-permute-start | bytes 2359304 | tf_op jit(solution)/shard_map/ppermute | solution.py:369
  153.1 18.4 %copy-start.7 = (f32[2,2,1,2,2,32,1024]{6,5,4,3,2,1,0:T(8,128)S(1)}, f32[2,2,1,2,2,32,1024]{6,5,4,3,2,1,0:T(8,128)}, u32[]{:S(2)}) copy-start(f32[2,2,1,2,2,32,1024]{6,5,4,3,2,1,0:T(8,128)} %get-tuple-element.12) | copy-start | bytes 6291460
  153.3 33.9 %collective-permute-start.5 = (bf16[2,512,384]{2,1,0:T(8,128)(2,1)S(1)}, bf16[2,512,384]{2,1,0:T(8,128)(2,1)S(1)}, u32[]{:S(2)}, u32[]{:S(2)}) collective-permute-start(bf16[2,512,384]{2,1,0:T(8,128)(2,1)S(1)} %get-tuple-element.17), channel_id=1, source_target_pairs={{1,0},{2,1},{3,2},{5,4},{6,5},{7,6},{9,8},{10,9},{11,10},{13,12},{... | collective-permute-start | bytes 2359304 | tf_op jit(solution)/shard_map/ppermute | solution.py:369
  154.7 33.7 %collective-permute-start.4 = (bf16[2,512,384]{2,1,0:T(8,128)(2,1)S(1)}, bf16[2,512,384]{2,1,0:T(8,128)(2,1)S(1)}, u32[]{:S(2)}, u32[]{:S(2)}) collective-permute-start(bf16[2,512,384]{2,1,0:T(8,128)(2,1)S(1)} %get-tuple-element.16), channel_id=1, source_target_pairs={{0,1},{1,2},{2,3},{4,5},{5,6},{6,7},{8,9},{9,10},{10,11},{12,13},{... | collective-permute-start | bytes 2359304 | tf_op jit(solution)/shard_map/ppermute | solution.py:369
  171.5 9.5 %copy-start.6 = (f32[2,2,2,2,2,32,1024]{6,5,4,3,2,1,0:T(8,128)S(1)}, f32[2,2,2,2,2,32,1024]{6,5,4,3,2,1,0:T(8,128)}, u32[]{:S(2)}) copy-start(f32[2,2,2,2,2,32,1024]{6,5,4,3,2,1,0:T(8,128)} %get-tuple-element.6) | copy-start | bytes 12582916
  173.8 17.9 %collective-permute-start.12 = (bf16[2,2,2,32,1024]{4,3,1,2,0:T(8,128)(2,1)S(1)}, bf16[2,2,2,32,1024]{4,3,1,2,0:T(8,128)(2,1)S(1)}, u32[]{:S(2)}, u32[]{:S(2)}) collective-permute-start(bf16[2,2,2,32,1024]{4,3,1,2,0:T(8,128)(2,1)S(1)} %fusion.11), channel_id=1, source_target_pairs={{0,16},{4,20},{8,24},{12,28},{16,0},{20,4},{24,8},{28,12},{1,17},{... | collective-permute-start | bytes 1572872 | tf_op jit(solution)/shard_map/ppermute | solution.py:401
  183.1 13.7 %collective-permute-start.7 = (bf16[2,2,2,32,1024]{4,3,2,1,0:T(8,128)(2,1)S(1)}, bf16[2,2,2,32,1024]{4,3,2,1,0:T(8,128)(2,1)S(1)}, u32[]{:S(2)}, u32[]{:S(2)}) collective-permute-start(bf16[2,2,2,32,1024]{4,3,2,1,0:T(8,128)(2,1)S(1)} %fusion.10), channel_id=1, source_target_pairs={{0,8},{4,12},{8,0},{12,4},{16,24},{20,28},{24,16},{28,20},{1,9},{5... | collective-permute-start | bytes 1572872 | tf_op jit(solution)/shard_map/ppermute | solution.py:401
  191.9 11.8 %collective-permute-start.13 = (bf16[2,2,32,1024]{3,2,0,1:T(8,128)(2,1)S(1)}, bf16[2,2,32,1024]{3,2,0,1:T(8,128)(2,1)S(1)}, u32[]{:S(2)}, u32[]{:S(2)}) collective-permute-start(bf16[2,2,32,1024]{3,2,0,1:T(8,128)(2,1)S(1)} %fusion.13), channel_id=1, source_target_pairs={{0,8},{4,12},{8,0},{12,4},{16,24},{20,28},{24,16},{28,20},{1,9},{5... | collective-permute-start | bytes 786440 | tf_op jit(solution)/shard_map/ppermute | solution.py:401
  197.1 9.3 %collective-permute-start.8 = (bf16[2,2,32,1024]{3,2,1,0:T(8,128)(2,1)S(1)}, bf16[2,2,32,1024]{3,2,1,0:T(8,128)(2,1)S(1)}, u32[]{:S(2)}, u32[]{:S(2)}) collective-permute-start(bf16[2,2,32,1024]{3,2,1,0:T(8,128)(2,1)S(1)} %fusion.12), channel_id=1, source_target_pairs={{0,16},{4,20},{8,24},{12,28},{16,0},{20,4},{24,8},{28,12},{1,17},{... | collective-permute-start | bytes 786440 | tf_op jit(solution)/shard_map/ppermute | solution.py:401
  203.9 6.9 %collective-permute-start.14 = (bf16[2,32,1024]{2,1,0:T(8,128)(2,1)S(1)}, bf16[2,32,1024]{2,1,0:T(8,128)(2,1)S(1)}, u32[]{:S(2)}, u32[]{:S(2)}) collective-permute-start(bf16[2,32,1024]{2,1,0:T(8,128)(2,1)S(1)} %fusion.15), channel_id=1, source_target_pairs={{0,1},{1,0},{2,3},{3,2},{4,5},{5,4},{6,7},{7,6},{8,9},{9,8},{10,11... | collective-permute-start | bytes 393224 | tf_op jit(solution)/shard_map/ppermute | solution.py:401
  206.4 14.0 %copy-start.1 = (bf16[1024,1024]{1,0:T(8,128)(2,1)S(1)}, bf16[1024,1024]{1,0:T(8,128)(2,1)}, u32[]{:S(2)}) copy-start(bf16[1024,1024]{1,0:T(8,128)(2,1)} %param.10) | copy-start | bytes 6291460
  206.5 7.8 %collective-permute-start.9 = (bf16[2,32,1024]{2,1,0:T(8,128)(2,1)S(1)}, bf16[2,32,1024]{2,1,0:T(8,128)(2,1)S(1)}, u32[]{:S(2)}, u32[]{:S(2)}) collective-permute-start(bf16[2,32,1024]{2,1,0:T(8,128)(2,1)S(1)} %fusion.14), channel_id=1, source_target_pairs={{0,1},{1,0},{2,3},{3,2},{4,5},{5,4},{6,7},{7,6},{8,9},{9,8},{10,11... | collective-permute-start | bytes 393224 | tf_op jit(solution)/shard_map/ppermute | solution.py:401
  210.8 7.6 %collective-permute-start.15 = (bf16[32,1024]{1,0:T(8,128)(2,1)S(1)}, bf16[32,1024]{1,0:T(8,128)(2,1)S(1)}, u32[]{:S(2)}, u32[]{:S(2)}) collective-permute-start(bf16[32,1024]{1,0:T(8,128)(2,1)S(1)} %fusion.17), channel_id=1, source_target_pairs={{0,2},{1,3},{2,0},{3,1},{4,6},{5,7},{6,4},{7,5},{8,10},{9,11},{10,... | collective-permute-start | bytes 196616 | tf_op jit(solution)/shard_map/ppermute | solution.py:401
  214.4 5.2 %collective-permute-start.10 = (bf16[32,1024]{1,0:T(8,128)(2,1)S(1)}, bf16[32,1024]{1,0:T(8,128)(2,1)S(1)}, u32[]{:S(2)}, u32[]{:S(2)}) collective-permute-start(bf16[32,1024]{1,0:T(8,128)(2,1)S(1)} %fusion.16), channel_id=1, source_target_pairs={{0,2},{1,3},{2,0},{3,1},{4,6},{5,7},{6,4},{7,5},{8,10},{9,11},{10,... | collective-permute-start | bytes 196616 | tf_op jit(solution)/shard_map/ppermute | solution.py:401
  (2 other events, 3.4 us)

commit v3 on v2

--- a/solution.py
+++ b/solution.py
@@ -426,6 +426,218 @@
     return jnp.concatenate([first, second], axis=0).reshape(-1)
 
 
+def flip(v, weights):
+    for w in weights:
+        v = v + w * (1 - 2 * ((v // w) % 2))
+    return v
+
+
+def finish_kernel(
+    n_ky, n_kx, rim, frame, term, grad, pupil,
+    got, acc, out_buf, in_buf, ring_u, ring_d, sides, ring_l, ring_r,
+    core_send, core_recv, red_send, red_recv, rim_send, rim_recv, side_send, side_recv,
+):
+    t = grad.shape[1]
+    ky, kx = lax.axis_index("ky"), lax.axis_index("kx")
+    pair, core = ky // 2, ky % 2
+    half = term.shape[3] // 2
+    bits_y = [("ky", 1 << k) for k in range((n_ky // 2).bit_length() - 1)]
+    bits_x = [("kx", 1 << k) for k in range(n_kx.bit_length() - 1)]
+    bits = bits_y + bits_x
+    orders = [bits_y + bits_x, bits_y[::-1] + bits_x[::-1]]
+    n_slots = 1 << len(bits)
+
+    def slot_bits(d):
+        return [b for i, b in enumerate(bits) if (d >> i) & 1]
+
+    def stage_of(d, h):
+        on = slot_bits(d)
+        for s, b in enumerate(orders[h]):
+            if b in on:
+                return s
+        return len(bits)
+
+    has = {"u": ky > 0, "d": ky < n_ky - 1, "l": kx > 0, "r": kx < n_kx - 1}
+    dev = {"u": (ky - 1, kx), "d": (ky + 1, kx), "l": (ky, kx - 1), "r": (ky, kx + 1)}
+    back = {"u": "d", "d": "u", "l": "r", "r": "l"}
+    mate = (flip(ky, [1]), kx)
+
+    def peer(b):
+        return (2 * flip(pair, [b[1]]) + core, kx) if b[0] == "ky" else (ky, flip(kx, [b[1]]))
+
+    always = ky >= 0
+    greet([(has[k], dev[k]) for k in "udlr"] + [(always, mate)] + [(always, peer(b)) for b in bits])
+
+    def place(d):
+        on = slot_bits(d)
+        return flip(pair, [w for n, w in on if n == "ky"]), flip(kx, [w for n, w in on if n == "kx"])
+
+    def core_copy(d):
+        g, c = place(d)
+        return remote(term.at[g, 1 - core, c], got.at[d], core_send.at[d], core_recv.at[d], mate)
+
+    def red_copy(h, d):
+        b = orders[h][stage_of(d, h)]
+        i = h * n_slots + d
+        return remote(out_buf.at[i], in_buf.at[i], red_send.at[i], red_recv.at[i], peer(b))
+
+    cols = [pl.ds(0, rim), pl.ds(rim + t, rim), pl.ds(rim, t)]
+
+    def rim_copy(q, k, p):
+        i = q * 6 + "ud".index(k) * 3 + p
+        rows = pl.ds(0, rim) if k == "u" else pl.ds(rim + t, rim)
+        dst = ring_d if k == "u" else ring_u
+        return remote(frame.at[q, rows, cols[p]], dst.at[q, :, cols[p]], rim_send.at[i], rim_recv.at[i], dev[k])
+
+    def side_copy(q, k):
+        i = q * 2 + "lr".index(k)
+        dst = ring_r if k == "l" else ring_l
+        return remote(sides.at[q, "lr".index(k)], dst.at[q], side_send.at[i], side_recv.at[i], dev[k])
+
+    order = sorted(range(n_slots), key=lambda d: (stage_of(d, 0) + stage_of(d, 1), d))
+    for d in order:
+        core_copy(d).start()
+    for q in range(2):
+        for p in range(2):
+            for k in "ud":
+                @pl.when(has[k])
+                def _(q=q, k=k, p=p):
+                    rim_copy(q, k, p).start()
+    for k, ring in (("u", ring_u), ("d", ring_d), ("l", ring_l), ("r", ring_r)):
+        @pl.when(jnp.logical_not(has[k]))
+        def _(ring=ring):
+            ring[...] = jnp.zeros(ring.shape, ring.dtype)
+
+    def push(h, d, value):
+        i = h * n_slots + d
+        if d == 0:
+            return
+        out_buf[i] = value.astype(BF)
+        red_copy(h, d).start()
+
+    for d in order:
+        core_copy(d).wait_recv()
+        g, c = place(d)
+        for h in range(2):
+            rows = pl.ds(h * half, half)
+            x = term[g, core, c, rows, :] + got[d, rows, :]
+            if stage_of(d, h) == 0:
+                push(h, d, x)
+            else:
+                acc[h * n_slots + d] = x
+    for q in range(2):
+        for k in "ud":
+            @pl.when(has[k])
+            def _(q=q, k=k):
+                rim_copy(q, k, 2).start()
+    for q in range(2):
+        for p in range(2):
+            for k in "ud":
+                @pl.when(has[k])
+                def _(q=q, k=k, p=p):
+                    rim_copy(q, back[k], p).wait_recv()
+            k = "lr"[p]
+            mid = rim - (t - rim)
+            for lo, n in ((0, t - rim), (t - rim, mid), (rim, t - rim)):
+                x = frame[q, rim + lo : rim + lo + n, cols[p]].astype(F32)
+                if lo < rim:
+                    x = x + ring_u[q, lo : lo + n, cols[p]].astype(F32)
+                if lo >= t - rim:
+                    x = x + ring_d[q, lo - (t - rim) : lo - (t - rim) + n, cols[p]].astype(F32)
+                sides[q, p, lo : lo + n, :] = x.astype(BF)
+
+            @pl.when(has[k])
+            def _(q=q, k=k):
+                side_copy(q, k).start()
+    for s in range(len(bits)):
+        for h in range(2):
+            for d in order:
+                b = orders[h][s]
+                before = [bits.index(v) for v in orders[h][: s + 1]]
+                if any((d >> i) & 1 for i in before):
+                    continue
+                i = h * n_slots + d
+                src = d ^ (1 << bits.index(b))
+                red_copy(h, src).wait_recv()
+                x = acc[i] + in_buf[h * n_slots + src].astype(F32)
+                if stage_of(d, h) == s + 1 and d != 0:
+                    push(h, d, x)
+                elif d != 0:
+                    acc[i] = x
+                elif s < len(bits) - 1:
+                    acc[i] = x
+                else:
+                    pupil[pl.ds(h * half, half), :] = x
+    gap = t - rim
+    for q in range(2):
+        for k in "ud":
+            @pl.when(has[k])
+            def _(q=q, k=k):
+                rim_copy(q, back[k], 2).wait_recv()
+        for lo, n in ((0, gap), (gap, rim - gap), (rim, gap)):
+            x = frame[q, rim + lo : rim + lo + n, cols[2]].astype(F32)
+            if lo < rim:
+                x = x + ring_u[q, lo : lo + n, cols[2]].astype(F32)
+            if lo >= gap:
+                x = x + ring_d[q, lo - gap : lo - gap + n, cols[2]].astype(F32)
+            grad[q, lo : lo + n, :] = x
+        for k in "lr":
+            @pl.when(has[k])
+            def _(q=q, k=k):
+                side_copy(q, back[k]).wait_recv()
+        grad[q, :, :rim] += ring_l[q].astype(F32)
+        grad[q, :, gap:] += ring_r[q].astype(F32)
+    for d in range(n_slots):
+        core_copy(d).wait_send()
+        if d:
+            for h in range(2):
+                red_copy(h, d).wait_send()
+    for q in range(2):
+        for k in "ud":
+            @pl.when(has[k])
+            def _(q=q, k=k):
+                for p in range(3):
+                    rim_copy(q, k, p).wait_send()
+        for k in "lr":
+            @pl.when(has[k])
+            def _(q=q, k=k):
+                side_copy(q, k).wait_send()
+
+
+def finish(frame, term, t, rim):
+    n_ky, n_kx = lax.axis_size("ky"), lax.axis_size("kx")
+    rows = 2 * WIN // (n_ky * n_kx)
+    n_slots = n_ky * n_kx // 2
+    side = frame.shape[1]
+    vm = pl.BlockSpec(memory_space=pltpu.VMEM)
+    dma = pltpu.SemaphoreType.DMA
+    grad, pupil = pl.pallas_call(
+        functools.partial(finish_kernel, n_ky, n_kx, rim),
+        out_shape=(jax.ShapeDtypeStruct((2, t, t), F32), jax.ShapeDtypeStruct((rows, WIN), F32)),
+        in_specs=[vm, vm],
+        out_specs=(vm, vm),
+        scratch_shapes=[
+            pltpu.VMEM((n_slots, rows, WIN), F32),
+            pltpu.VMEM((2 * n_slots, rows // 2, WIN), F32),
+            pltpu.VMEM((2 * n_slots, rows // 2, WIN), BF),
+            pltpu.VMEM((2 * n_slots, rows // 2, WIN), BF),
+            pltpu.VMEM((2, rim, side), BF),
+            pltpu.VMEM((2, rim, side), BF),
+            pltpu.VMEM((2, 2, t, rim), BF),
+            pltpu.VMEM((2, t, rim), BF),
+            pltpu.VMEM((2, t, rim), BF),
+            dma((n_slots,)), dma((n_slots,)),
+            dma((2 * n_slots,)), dma((2 * n_slots,)),
+            dma((12,)), dma((12,)),
+            dma((4,)), dma((4,)),
+        ],
+        compiler_params=pltpu.CompilerParams(
+            collective_id=1, has_side_effects=True, vmem_limit_bytes=60 * 1024 * 1024
+        ),
+    )(frame, term.reshape(n_ky // 2, 2, n_kx, rows, WIN))
+    return grad, pupil.reshape(-1)
+
+
 def body(spectrum, pupil_field, amplitude, offsets):
     t = spectrum.shape[1]
     rim = 3 * t // 4
@@ -440,9 +652,9 @@
     region = gather_region(spectrum, rim)
     n_leds = lax.axis_size("ky") * lax.axis_size("kx")
     frame, term = compute(starts, region, pupil_field, amp, n_leds)
-    pupil_grad = reduce_terms(term)
-    spectrum_grad = scatter_frame(frame, t, rim)
-    return (spectrum_grad, pupil_grad)
+    if n_leds == 32:
+        return finish(frame, term, t, rim)
+    return (scatter_frame(frame, t, rim), reduce_terms(term))
 
 
 def solution(mesh):

time: 221 us -> 204 us (0.923)
  Pallas kernels: 80.3 us -> 186 us
  starting transfers between devices: 77.4 us -> 0 us
  waiting for transfers between devices: 17.5 us -> 0 us
  local copies, waits for them, and re-layouts: 24.6 us -> 8.86 us
  other arithmetic: 12.2 us -> 0.65 us
    pallas_call x0 -> x1, Pallas kernels: none -> 106 us  [finish(): pl.pallas_call(functools.partial(finish_kernel, n_ky, n_kx, rim), out_sha...]
    ppermute x16 -> x0, starting transfers between devices: 77.4 us -> none  [the longest x6 43.9 us: shift(): return lax.ppermute(x, axis, pairs)]
    ppermute x16 -> x0, waiting for transfers between devices: 17.5 us -> none  [the longest x10 12.3 us: halve(): got = lax.ppermute(send, axis, [(i, i ^ weight) for i in range(n)])]
    slice x4 -> x0, local copies, waits for them, and re-layouts: 10.2 us -> none  [the longest x1 8.43 us: reduce_terms(): first = chain(flat[..., :half, :], core + y_bits + x_bits)]
    add x11 -> x0, other arithmetic: 7.97 us -> none  [the longest x10 4.64 us: halve(): return keep + got.astype(F32)]
    dynamic_slice x2 -> x0, local copies, waits for them, and re-layouts: 5.87 us -> none  [the longest x1 4.28 us: halve(): keep = lax.dynamic_index_in_dim(x, bit, dim, keepdims=False)]
    unnamed x21 -> x8, local copies, waits for them, and re-layouts: 5.25 us -> 7.46 us
  transfers between devices with their start and end apart: 16 -> 0, of which waited for: 6 -> 0; matrix products, arithmetic and copies ran while one was open for 7% -> 0% of each run, Pallas kernels for 0% -> 0%
where the time goes in v3:
time: 204 us
  Pallas kernels  186 us (91%)
  local copies, waits for them, and re-layouts  8.86 us (4%)
  matrix products  5.93 us (3%)
    pallas_call x1, Pallas kernels, finish(): pl.pallas_call(functools.partial(finish_kernel, n_ky, n_kx, rim), out_sha...  106 us
    pallas_call x1, Pallas kernels, compute(): pl.pallas_call(functools.partial(kernel, 1.0 / n_leds), out_shape=(jax.Sh...  56.5 us
    pallas_call x1, Pallas kernels, gather_region(): pl.pallas_call(functools.partial(halo_kernel, lax.axis_size('ky'), lax.ax...  23.8 us
    unnamed x8, local copies, waits for them, and re-layouts  7.46 us
    dot_general x1, matrix products, body(): amp = jnp.dot(amp, pick.T, preferred_element_type=F32).astype(BF)  5.93 us

profile of v3, /device:TPU:0, one launch (start us, length us, event | category | flops | bytes accessed | tf_op | source)
XLA Modules:
  0.0 203.8 jit_solution(1489790111773681792)
XLA Ops:
  0.6 0.0 copy-start
  0.7 1.4 fusion.17
  3.4 0.6 pad_add_fusion.starts
  4.0 0.0 copy-done
  4.0 0.0 copy-start.2
  4.0 5.9 %fusion.5.amp = bf16[1024,1024]{1,0:T(8,128)(2,1)} fusion(s32[1024]{0:T(1024)S(1)} %fusion.14, bf16[1024,1024]{1,0:T(8,128)(2,1)S(1)} %copy-done), kind=kOutput, calls=%fused_computation.6 | convolution fusion | flops 4299161600 | bytes 4198400 | tf_op jit(solution)/shard_map/dot_general | solution.py:651
  9.9 0.0 copy-done.2
  9.9 23.8 %shard_map.95.region = bf16[2,1280,1280]{2,1,0:T(8,128)(2,1)S(1)} custom-call(bf16[2,512,512]{2,1,0:T(8,128)(2,1)S(1)} %copy-done.2), custom_call_target="tpu_custom_call" | custom-call | tf_op jit(solution)/shard_map/pallas_call | solution.py:354
  33.8 0.0 copy-start.1
  33.8 2.7 %copy-done.1 = bf16[2,1280,1280]{2,1,0:T(8,128)(2,1)} copy-done((bf16[2,1280,1280]{2,1,0:T(8,128)(2,1)}, bf16[2,1280,1280]{2,1,0:T(8,128)(2,1)S(1)}, u32[]{:S(2)}) %copy-start.1) | copy-done | bytes 6553624
  36.5 56.5 %shard_map.96 = (bf16[2,1280,1280]{2,1,0:T(8,128)(2,1)}, f32[2,1024,1024]{2,1,0:T(8,128)}) custom-call(s32[2]{0:T(128)} %pad_add_fusion.starts, bf16[2,1280,1280]{2,1,0:T(8,128)(2,1)} %copy-done.1, bf16[2,1024,1024]{2,1,0:T(8,128)(2,1)} %pupil.1, bf16[1024,1024]{1,0:T(8,128)(2,1)} %fusion.5.amp, bf16[2,768,256]{2,1,0:T(8,128)(2,1)} %constant.56.clone.lane_t, ...), custom_call_target="tpu_custom_call" | custom-call | flops 12999999488 | bytes 30000000 | tf_op jit(solution)/shard_map/pallas_call | solution.py:238
  93.0 106.0 %shard_map.97 = (f32[2,512,512]{2,1,0:T(8,128)}, f32[64,1024]{1,0:T(8,128)}) custom-call(bf16[2,1280,1280]{2,1,0:T(8,128)(2,1)} %get-tuple-element.6.frame, f32[4,2,4,64,1024]{4,3,2,1,0:T(8,128)} %bitcast.8), custom_call_target="tpu_custom_call" | custom-call | tf_op jit(solution)/shard_map/pallas_call | solution.py:614
  199.0 1.7 copy.10
  200.7 3.1 %copy.12 = f32[2,512,512]{2,1,0:T(8,128)} copy(f32[2,512,512]{2,1,0:T(8,128)} %get-tuple-element.14) | data formatting | bytes 4194304
  (1 shorter events, 0.0 us)
Async XLA Ops:
  0.6 3.4 %copy-start = (bf16[1024,1024]{1,0:T(8,128)(2,1)S(1)}, bf16[1024,1024]{1,0:T(8,128)(2,1)}, u32[]{:S(2)}) copy-start(bf16[1024,1024]{1,0:T(8,128)(2,1)} %param.10) | copy-start | bytes 6291460
  4.0 5.9 %copy-start.2 = (bf16[2,512,512]{2,1,0:T(8,128)(2,1)S(1)}, bf16[2,512,512]{2,1,0:T(8,128)(2,1)}, u32[]{:S(2)}) copy-start(bf16[2,512,512]{2,1,0:T(8,128)(2,1)} %tile.1) | copy-start | bytes 3145732
  33.8 2.7 %copy-start.1 = (bf16[2,1280,1280]{2,1,0:T(8,128)(2,1)}, bf16[2,1280,1280]{2,1,0:T(8,128)(2,1)S(1)}, u32[]{:S(2)}) copy-start(bf16[2,1280,1280]{2,1,0:T(8,128)(2,1)S(1)} %shard_map.95.region) | copy-start | bytes 19660804
